TPU v7x, 128 devices: a whole 4x4x4 slice. The times are simulated.
128 devices in a mesh: dp: 32 (over z, x, core), seq: 4 (over y).
Axes of the slice: x: 4, y: 4, z: 4, core: 2. Of those that a mesh axis runs over, the one named last changes fastest.
Arguments:
- glu_out: bfloat16 [64, 2048, 1536], P('dp', 'seq'), may hold values from -6 to 6
- lengths: int32 [64, 8], P('dp'), may hold values from 1 to 512, 2048 in all within a row
- kernel: float32 [31, 1536], replicated, may hold values from -1 to 1
- norm_gain: float32 [1536], replicated, may hold values from 0.1 to 1.9
- norm_bias: float32 [1536], replicated, may hold values from -3 to 3
- w_out: bfloat16 [1536, 1536], replicated, may hold values from -0.15625 to 0.15625
- cotangent: bfloat16 [64, 2048, 1536], P('dp', 'seq'), may hold values from -6 to 6
Outputs:
- layer_out: bfloat16 [64, 2048, 1536], P('dp', 'seq')
- grad_input: bfloat16 [64, 2048, 1536], P('dp', 'seq')
- grad_w_out: float32 [1536, 1536], P('seq')
- grad_kernel: float32 [31, 1536], replicated
- grad_gain: float32 [1536], replicated
- grad_bias: float32 [1536], replicated
Inputs may be any that keep to these rules, and one draw needn't show every extreme that they name: Each lane's 8 utterance lengths sum to 2048, and the longest is exactly 512 frames.
All inputs are finite; a program needn't handle non-finite values.
Results may differ from a plain program's by a relative error of at most 0.0049.
Values may be sent and summed in bfloat16 or wider, within the bound.
No kernel may reach another device: no remote copies, remote signals or barrier semaphores. Data moves between devices by JAX's collectives and lax.ppermute only.
A program may use at most 128 MiB of HBM per device.

v0:
```python
import math

import jax
import jax.numpy as jnp
from jax import lax
from jax.sharding import PartitionSpec as P

EPSILON = 1e-05


def padded_2(array, sides, width):
    for axis, dim in sides:
        size, length = (lax.axis_size(axis), array.shape[dim])
        up = [(i, (i + 1) % size) for i in range(size - 1)]
        down = [(j, i) for i, j in up]
        last = lax.slice_in_dim(array, length - width, length, axis=dim)
        leading = lax.slice_in_dim(array, 0, width, axis=dim)
        before = lax.ppermute(last, axis, up)
        after = lax.ppermute(leading, axis, down)
        array = jnp.concatenate([before, array, after], axis=dim)
    return array


def segment_of(lengths, positions):
    utter_ends = jnp.cumsum(lengths, axis=-1)
    return jnp.sum((utter_ends[..., None, :] <= positions[:, None]).astype(jnp.int32), axis=-1)


def local(glu_out, lengths, kernel, norm_gain, norm_bias, w_out, cotangent):
    lane_count, slab_rows, channels = glu_out.shape
    taps = kernel.shape[0]
    half_width = taps // 2
    seq_count = lax.axis_size("seq")
    time_len = slab_rows * seq_count
    norm_scale = 1.0 / math.sqrt(lane_count * lax.axis_size("dp") * time_len)
    seq_place = lax.axis_index("seq")
    positions = (
        seq_place * slab_rows - half_width + jnp.arange(slab_rows + 2 * half_width, dtype=jnp.int32)
    )
    inside = (positions >= 0) & (positions < time_len)
    segment = jnp.where(inside[None, :], segment_of(lengths, positions), -1)
    own_segment = segment[:, half_width : half_width + slab_rows]
    padded = padded_2(glu_out, (("seq", 1),), half_width)
    conv = jnp.zeros((lane_count, slab_rows, channels), jnp.float32)
    for offset in range(taps):
        match = (segment[:, offset : offset + slab_rows] == own_segment).astype(jnp.float32)[
            ..., None
        ]
        conv = (
            conv
            + kernel[offset] * padded[:, offset : offset + slab_rows].astype(jnp.float32) * match
        )
    average = jnp.mean(conv, axis=-1, keepdims=True)
    centred = conv - average
    variance = jnp.mean(centred * centred, axis=-1, keepdims=True)
    inv_std = lax.rsqrt(variance + EPSILON)
    normed = centred * inv_std
    affine = normed * norm_gain + norm_bias
    gate_sigmoid = jax.nn.sigmoid(affine)
    swished = (affine * gate_sigmoid).astype(jnp.bfloat16)
    swished_rows = swished.reshape(-1, channels)
    cot_rows = cotangent.reshape(-1, channels)
    layer_out = jnp.dot(swished_rows, w_out, preferred_element_type=jnp.float32).astype(
        jnp.bfloat16
    )
    layer_out = layer_out.reshape(lane_count, slab_rows, channels)
    share_rows = channels // seq_count
    local_outer = lax.dot_general(
        swished_rows, cot_rows, (((0,), (0,)), ((), ())), preferred_element_type=jnp.float32
    )
    summed_outer = lax.psum(local_outer, ("dp", "seq"))
    grad_w_out = (
        lax.dynamic_slice_in_dim(summed_outer, seq_place * share_rows, share_rows, 0) * norm_scale
    )
    grad_swish = lax.dot_general(
        cot_rows, w_out, (((1,), (1,)), ((), ())), preferred_element_type=jnp.float32
    )
    grad_swish = grad_swish.reshape(lane_count, slab_rows, channels)
    grad_affine = grad_swish * gate_sigmoid * (1.0 + affine * (1.0 - gate_sigmoid))
    local_gain = jnp.sum(grad_affine * normed, axis=(0, 1))
    local_bias = jnp.sum(grad_affine, axis=(0, 1))
    grad_normed = grad_affine * norm_gain
    grad_conv = inv_std * (
        grad_normed
        - jnp.mean(grad_normed, axis=-1, keepdims=True)
        - normed * jnp.mean(grad_normed * normed, axis=-1, keepdims=True)
    )
    grad_pad = padded_2(grad_conv, (("seq", 1),), half_width)
    grad_lane = jnp.zeros((lane_count, slab_rows, channels), jnp.float32)
    kernel_rows = []
    for offset in range(taps):
        back_index = 2 * half_width - offset
        back_match = (segment[:, back_index : back_index + slab_rows] == own_segment).astype(
            jnp.float32
        )[..., None]
        grad_lane = (
            grad_lane
            + kernel[offset] * grad_pad[:, back_index : back_index + slab_rows] * back_match
        )
        match = (segment[:, offset : offset + slab_rows] == own_segment).astype(jnp.float32)[
            ..., None
        ]
        kernel_rows.append(
            jnp.sum(
                grad_conv * padded[:, offset : offset + slab_rows].astype(jnp.float32) * match,
                axis=(0, 1),
            )
        )
    local_kernel = jnp.stack(kernel_rows, axis=0)
    grad_input = grad_lane.astype(jnp.bfloat16)
    summed_kernel, summed_gain, summed_bias = lax.psum(
        (local_kernel, local_gain, local_bias), ("dp", "seq")
    )
    return (
        layer_out,
        grad_input,
        grad_w_out,
        summed_kernel * norm_scale,
        summed_gain * norm_scale,
        summed_bias * norm_scale,
    )


def solution(mesh):
    in_specs = (P("dp", "seq", None), P("dp", None), P(), P(), P(), P(), P("dp", "seq", None))
    out_specs = (P("dp", "seq", None), P("dp", "seq", None), P("seq", None), P(), P(), P())
    return jax.shard_map(local, mesh=mesh, in_specs=in_specs, out_specs=out_specs, check_vma=False)
```

profile of v0, /device:TPU:1, one launch (start us, length us, event | category | flops | bytes accessed | tf_op | source)
XLA Modules:
  0.0 459.6 jit_solution(8754268860323534279)
XLA Ops:
  7.2 1.8 fusion.261
  9.1 4.0 collective-permute-start
  13.1 1.3 collective-permute-start.1
  14.4 0.9 reduce_window_sum.11
  15.4 0.7 compare_convert_fusion.26
  16.1 0.7 compare_convert_fusion.27
  16.8 0.7 compare_convert_fusion.28
  17.5 0.7 compare_convert_fusion.29
  18.2 3.8 constant_dynamic-update-slice_fusion.1
  22.0 0.9 slice_reduce_fusion.30
  23.2 0.6 constant_dynamic-update-slice_fusion
  23.9 81.3 %fusion.258 = (f32[2,512]{1,0:T(2,128)S(1)}, f32[2,512,1536]{2,1,0:T(8,128)}) fusion(f32[2,512]{1,0:T(2,128)} %get-tuple-element.113, bf16[2,527,1536]{2,1,0:T(8,128)(2,1)} %constant_dynamic-update-slice_fusion, f32[1536]{0:T(1024)S(1)} %get-tuple-element.70, f32[2,512]{1,0:T(2,128)} %get-tuple-element.85, f32[1536]{0:T(1024)S(1)} %get-tuple-element.71, ...), kind=kLoop, calls=%fused_computation.473 | loop fusion | flops 264240128 | bytes 57032704 | tf_op jit(solution)/shard_map/reduce_sum | solution.py:53
  105.4 3.7 multiply_reduce_fusion.2
  109.1 0.8 copy-done.4
  110.0 13.2 %multiply_reduce_fusion = (f32[1536]{0:T(1024)}, f32[2,512]{1,0:T(2,128)S(1)}, f32[2,512]{1,0:T(2,128)S(1)}, f32[1536]{0:T(1024)}, bf16[2,512,1536]{2,1,0:T(8,128)(2,1)}, /*index=5*/f32[2,512,1536]{2,1,0:T(8,128)S(1)}) fusion(f32[2,512,1536]{2,1,0:T(8,128)S(1)} %copy-done.4, f32[2,512]{1,0:T(2,128)S(1)} %add_rsqrt_fusion, ...), kind=kOutput, calls=%fused_computation.370 | convolution fusion | flops 4864863232 | bytes 23633920 | tf_op jit(solution)/shard_map/dot_general | solution.py:75
  123.3 14.2 %fusion.120 = (f32[1536]{0:T(1024)S(1)}, f32[1536]{0:T(1024)S(1)}, f32[1536]{0:T(1024)S(1)}, f32[1536]{0:T(1024)S(1)}, f32[1536]{0:T(1024)S(1)}, /*index=5*/f32[...) fusion(f32[2,512]{1,0:T(2,128)S(1)} %copy-done.47, ...), kind=kLoop, calls=%fused_computation.225 | loop fusion | flops 67619328 | bytes 47300608 | tf_op jit(solution)/shard_map/reduce_sum | solution.py:104
  137.7 9.6 %fusion.117 = (f32[1536]{0:T(1024)S(1)}, f32[1536]{0:T(1024)S(1)}, f32[1536]{0:T(1024)S(1)}, f32[1536]{0:T(1024)S(1)}, f32[1536]{0:T(1024)S(1)}, /*index=5*/f32[1536]{0:T(1024)S(1)}) fusion(f32[2,512,1536]{2,1,0:T(8,128)S(1)} %get-tuple-element.76, f32[2,512]{1,0:T(2,128)S(1)} %copy-done.64, bf16[2,527,1536]{2,1,0:T(8,128)(2,1)S(1)} %copy-done.1, ...), kind=kLoop, calls=%fused_computation.222 | loop fusion | flops 37739520 | bytes 25227264 | tf_op jit(solution)/shard_map/reduce_sum | solution.py:104
  147.4 0.7 fusion.260
  157.0 5.0 %fusion.32 = (f32[1536]{0:T(1024)S(1)}, f32[1536]{0:T(1024)S(1)}, f32[1536]{0:T(1024)S(1)}, f32[1536]{0:T(1024)S(1)}) fusion(f32[2,512,1536]{2,1,0:T(8,128)S(1)} %get-tuple-element.76, f32[2,512]{1,0:T(2,128)S(1)} %copy-done.42, bf16[2,512,1536]{2,1,0:T(8,128)(2,1)S(1)} %copy-done.3, bf16[2,15,1536]{2,1,0:T(8,128)(2,1)S(1)} %collective-permute-done, ...), kind=kLoop, calls=%fused_computation.137 | loop fusion | flops 37742592 | bytes 9566208 | tf_op jit(solution)/shard_map/reduce_sum | solution.py:104
  164.5 10.6 %fusion.50 = (f32[1536]{0:T(1024)S(1)}, f32[1536]{0:T(1024)S(1)}, f32[1536]{0:T(1024)S(1)}, f32[1536]{0:T(1024)S(1)}, f32[1536]{0:T(1024)S(1)}, /*index=5*/f32[1536]{0:T(1024)S(1)}) fusion(f32[2,512,1536]{2,1,0:T(8,128)S(1)} %get-tuple-element.76, f32[2,512]{1,0:T(2,128)S(1)} %copy-done.52, bf16[2,512,1536]{2,1,0:T(8,128)(2,1)S(1)} %copy-done.3, ...), kind=kLoop, calls=%fused_computation.155 | loop fusion | flops 66051072 | bytes 9590784 | tf_op jit(solution)/shard_map/reduce_sum | solution.py:104
  175.8 8.7 %fusion.68 = (f32[1536]{0:T(1024)S(1)}, f32[1536]{0:T(1024)S(1)}, f32[1536]{0:T(1024)S(1)}, f32[1536]{0:T(1024)S(1)}, f32[1536]{0:T(1024)S(1)}, /*index=5*/f32[1536]{0:T(1024)S(1)}) fusion(f32[2,512,1536]{2,1,0:T(8,128)S(1)} %get-tuple-element.76, bf16[2,512,1536]{2,1,0:T(8,128)(2,1)S(1)} %copy-done.3, bf16[2,15,1536]{2,1,0:T(8,128)(2,1)S(1)} %collective-permute-done, ...), kind=kLoop, calls=%fused_computation.173 | loop fusion | flops 66051072 | bytes 9590784 | tf_op jit(solution)/shard_map/reduce_sum | solution.py:104
  191.0 1.3 collective-permute-start.2
  192.3 5.3 %collective-permute-start.3 = (f32[2,15,1536]{2,1,0:T(8,128)S(1)}, f32[2,15,1536]{2,1,0:T(8,128)}, u32[]{:S(2)}, u32[]{:S(2)}) collective-permute-start(f32[2,15,1536]{2,1,0:T(8,128)S(1)} %get-tuple-element.81), channel_id=1, source_target_pairs={{0,1},{1,2},{2,3},{4,5},{5,6},{6,7},{8,9},{9,10},{10,11},{12,13},{... | collective-permute-start | bytes 552968 | tf_op jit(solution)/shard_map/ppermute | solution.py:18
  197.6 7.8 %convolution_bitcast_fusion = f32[1536,1536]{1,0:T(8,128)} fusion(bf16[2,512,1536]{2,1,0:T(8,128)(2,1)S(1)} %copy-done.74, bf16[2,512,1536]{2,1,0:T(8,128)(2,1)S(1)} %copy-done), kind=kOutput, calls=%fused_computation.42 | convolution fusion | flops 4831838208 | bytes 15728640 | tf_op jit(solution)/shard_map/dot_general | solution.py:68
  205.4 6.4 %convolution_convert_fusion = bf16[1024,1536]{1,0:T(8,128)(2,1)} fusion(bf16[1024,1536]{1,0:T(8,128)(2,1)S(1)} %bitcast.19, bf16[1536,1536]{1,0:T(8,128)(2,1)S(1)} %bitcast.17), kind=kOutput, calls=%fused_computation.382 | convolution fusion | flops 4833411072 | bytes 11010048 | tf_op jit(solution)/shard_map/dot_general | solution.py:63
  212.0 68.1 %all-reduce = (f32[1536]{0:T(1024)}, f32[1536]{0:T(1024)}) all-reduce(f32[1536]{0:T(1024)} %get-tuple-element.6, f32[1536]{0:T(1024)} %get-tuple-element.40), channel_id=1, replica_groups=mesh['dp'=32,'seq'=4] {'dp','seq'}, use_global_device_ids=true, to_apply=%region_40.41 | all-reduce | flops 3072 | bytes 24576 | tf_op jit(solution)/shard_map/psum | solution.py:111
  280.1 6.0 %stack.127 = f32[31,1536]{1,0:T(8,128)} concatenate(f32[1,1536]{1,0:T(1,128)} %stack.96, f32[1,1536]{1,0:T(1,128)} %stack.97, f32[1,1536]{1,0:T(1,128)} %stack.98, f32[1,1536]{1,0:T(1,128)} %stack.99, f32[1,1536]{1,0:T(1,128)} %stack.100, f32[1,1536]{1,0:T(1,128)} %stack.101, f32[1,1536]{1,0:T(1,128)} %stack.102, f32[1,1536]{1,0:T(1,128)} %stack.103, f32[1,1536]{1,0:T(1,128)} %stack.104, ...), dimensions={0} | concatenate | bytes 380928 | tf_op jit(solution)/shard_map/stack | solution.py:109
  286.1 1.3 broadcast_multiply_fusion.1
  287.7 115.2 %fusion.126 = bf16[2,512,1536]{2,1,0:T(8,128)(2,1)} fusion(f32[2,15,1536]{2,1,0:T(8,128)} %collective-permute-done.3, f32[2,15,1536]{2,1,0:T(8,128)} %collective-permute-done.2, f32[2,512,1536]{2,1,0:T(8,128)} %copy-done.2, f32[2,512]{1,0:T(2,128)} %get-tuple-element.113, f32[1536]{0:T(1024)} %copy-done.40, f32[2,512]{1,0:T(2,128)} %get-tuple-element.85, ...), kind=kLoop, calls=%fused_computation.231 | loop fusion | flops 191889408 | bytes 10119168 | tf_op jit(solution)/shard_map/convert_element_type | solution.py:110
  402.9 45.0 %all-reduce.4.cloned.1.call-done = (f32[1536,1536]{1,0:T(8,128)}, f32[31,1536]{1,0:T(8,128)}) async-done(((f32[1536,1536]{1,0:T(8,128)}, f32[31,1536]{1,0:T(8,128)}), (f32[1536,1536]{1,0:T(8,128)}, f32[31,1536]{1,0:T(8,128)})) %all-reduce.4.cloned.1.call-update) | async-done | bytes 9627664 | tf_op jit(solution)/shard_map/psum | solution.py:71
  447.9 1.6 broadcast_multiply_fusion
  449.5 3.3 dynamic-slice_multiply_fusion
  (199 shorter events, 19.2 us)
Async XLA Ops:
  7.2 101.9 %copy-start = (bf16[2,512,1536]{2,1,0:T(8,128)(2,1)S(1)}, bf16[2,512,1536]{2,1,0:T(8,128)(2,1)}, u32[]{:S(2)}) copy-start(bf16[2,512,1536]{2,1,0:T(8,128)(2,1)} %param.13) | copy-start | bytes 9437188
  7.2 440.7 %all-reduce.4.cloned.1.call-start = ((), (), s32[]{:S(2)}) async-start(), calls=%async_computation | async-start | bytes 19267584 | tf_op jit(solution)/shard_map/psum | solution.py:71
  9.1 14.8 %collective-permute-start = (bf16[2,15,1536]{2,1,0:T(8,128)(2,1)}, bf16[2,15,1536]{2,1,0:T(8,128)(2,1)S(1)}, u32[]{:S(2)}, u32[]{:S(2)}) collective-permute-start(bf16[2,15,1536]{2,1,0:T(8,128)(2,1)} %get-tuple-element.82), channel_id=1, source_target_pairs={{0,1},{1,2},{2,3},{4,5},{5,6},{6,7},{8,9},{9,10},{10,11},{12,13},{... | collective-permute-start | bytes 276488 | tf_op jit(solution)/shard_map/ppermute | solution.py:18
  13.1 10.2 %collective-permute-start.1 = (bf16[2,15,1536]{2,1,0:T(8,128)(2,1)}, bf16[2,15,1536]{2,1,0:T(8,128)(2,1)S(1)}, u32[]{:S(2)}, u32[]{:S(2)}) collective-permute-start(bf16[2,15,1536]{2,1,0:T(8,128)(2,1)} %get-tuple-element.83), channel_id=1, source_target_pairs={{1,0},{2,1},{3,2},{5,4},{6,5},{7,6},{9,8},{10,9},{11,10},{13,12},{... | collective-permute-start | bytes 276488 | tf_op jit(solution)/shard_map/ppermute | solution.py:19
  23.1 82.1 %copy-start.23 = (f32[1536]{0:T(1024)}, f32[1536]{0:T(1024)S(1)}, u32[]{:S(2)}) copy-start(f32[1536]{0:T(1024)S(1)} %get-tuple-element.60) | copy-start | bytes 18436
  23.1 82.1 %copy-start.25 = (f32[1536]{0:T(1024)}, f32[1536]{0:T(1024)S(1)}, u32[]{:S(2)}) copy-start(f32[1536]{0:T(1024)S(1)} %get-tuple-element.61) | copy-start | bytes 18436
  23.1 82.1 %copy-start.27 = (f32[1536]{0:T(1024)}, f32[1536]{0:T(1024)S(1)}, u32[]{:S(2)}) copy-start(f32[1536]{0:T(1024)S(1)} %get-tuple-element.62) | copy-start | bytes 18436
  23.1 82.1 %copy-start.29 = (f32[1536]{0:T(1024)}, f32[1536]{0:T(1024)S(1)}, u32[]{:S(2)}) copy-start(f32[1536]{0:T(1024)S(1)} %get-tuple-element.63) | copy-start | bytes 18436
  23.2 82.1 %copy-start.31 = (f32[1536]{0:T(1024)}, f32[1536]{0:T(1024)S(1)}, u32[]{:S(2)}) copy-start(f32[1536]{0:T(1024)S(1)} %get-tuple-element.64) | copy-start | bytes 18436
  23.2 82.1 %copy-start.33 = (f32[1536]{0:T(1024)}, f32[1536]{0:T(1024)S(1)}, u32[]{:S(2)}) copy-start(f32[1536]{0:T(1024)S(1)} %get-tuple-element.65) | copy-start | bytes 18436
  23.2 82.1 %copy-start.35 = (f32[1536]{0:T(1024)}, f32[1536]{0:T(1024)S(1)}, u32[]{:S(2)}) copy-start(f32[1536]{0:T(1024)S(1)} %get-tuple-element.66) | copy-start | bytes 18436
  23.2 82.1 %copy-start.37 = (f32[1536]{0:T(1024)}, f32[1536]{0:T(1024)S(1)}, u32[]{:S(2)}) copy-start(f32[1536]{0:T(1024)S(1)} %get-tuple-element.67) | copy-start | bytes 18436
  23.2 82.1 %copy-start.38 = (f32[1536]{0:T(1024)}, f32[1536]{0:T(1024)S(1)}, u32[]{:S(2)}) copy-start(f32[1536]{0:T(1024)S(1)} %get-tuple-element.68) | copy-start | bytes 18436
  23.2 82.1 %copy-start.39 = (f32[1536]{0:T(1024)}, f32[1536]{0:T(1024)S(1)}, u32[]{:S(2)}) copy-start(f32[1536]{0:T(1024)S(1)} %get-tuple-element.69) | copy-start | bytes 18436
  23.2 82.1 %copy-start.40 = (f32[1536]{0:T(1024)}, f32[1536]{0:T(1024)S(1)}, u32[]{:S(2)}) copy-start(f32[1536]{0:T(1024)S(1)} %get-tuple-element.70) | copy-start | bytes 18436
  23.2 82.1 %copy-start.41 = (f32[1536]{0:T(1024)}, f32[1536]{0:T(1024)S(1)}, u32[]{:S(2)}) copy-start(f32[1536]{0:T(1024)S(1)} %get-tuple-element.71) | copy-start | bytes 18436
  191.0 96.4 %collective-permute-start.2 = (f32[2,15,1536]{2,1,0:T(8,128)}, f32[2,15,1536]{2,1,0:T(8,128)}, u32[]{:S(2)}, u32[]{:S(2)}) collective-permute-start(f32[2,15,1536]{2,1,0:T(8,128)} %get-tuple-element.80), channel_id=1, source_target_pairs={{1,0},{2,1},{3,2},{5,4},{6,5},{7,6},{9,8},{10,9},{11,10},{13,12},{... | collective-permute-start | bytes 552968 | tf_op jit(solution)/shard_map/ppermute | solution.py:19
  192.3 95.1 %collective-permute-start.3 = (f32[2,15,1536]{2,1,0:T(8,128)S(1)}, f32[2,15,1536]{2,1,0:T(8,128)}, u32[]{:S(2)}, u32[]{:S(2)}) collective-permute-start(f32[2,15,1536]{2,1,0:T(8,128)S(1)} %get-tuple-element.81), channel_id=1, source_target_pairs={{0,1},{1,2},{2,3},{4,5},{5,6},{6,7},{8,9},{9,10},{10,11},{12,13},{... | collective-permute-start | bytes 552968 | tf_op jit(solution)/shard_map/ppermute | solution.py:18
  211.8 75.7 %copy-start.10 = (f32[1536]{0:T(1024)S(1)}, f32[1536]{0:T(1024)}, u32[]{:S(2)}) copy-start(f32[1536]{0:T(1024)} %get-tuple-element.47) | copy-start | bytes 18436
  211.8 75.7 %copy-start.11 = (f32[1536]{0:T(1024)S(1)}, f32[1536]{0:T(1024)}, u32[]{:S(2)}) copy-start(f32[1536]{0:T(1024)} %get-tuple-element.48) | copy-start | bytes 18436
  211.8 75.7 %copy-start.12 = (f32[1536]{0:T(1024)S(1)}, f32[1536]{0:T(1024)}, u32[]{:S(2)}) copy-start(f32[1536]{0:T(1024)} %get-tuple-element.49) | copy-start | bytes 18436
  211.8 75.7 %copy-start.13 = (f32[1536]{0:T(1024)S(1)}, f32[1536]{0:T(1024)}, u32[]{:S(2)}) copy-start(f32[1536]{0:T(1024)} %get-tuple-element.50) | copy-start | bytes 18436
  211.8 75.7 %copy-start.14 = (f32[1536]{0:T(1024)S(1)}, f32[1536]{0:T(1024)}, u32[]{:S(2)}) copy-start(f32[1536]{0:T(1024)} %get-tuple-element.51) | copy-start | bytes 18436
  211.9 75.7 %copy-start.15 = (f32[1536]{0:T(1024)S(1)}, f32[1536]{0:T(1024)}, u32[]{:S(2)}) copy-start(f32[1536]{0:T(1024)} %get-tuple-element.52) | copy-start | bytes 18436
  211.9 75.7 %copy-start.16 = (f32[1536]{0:T(1024)S(1)}, f32[1536]{0:T(1024)}, u32[]{:S(2)}) copy-start(f32[1536]{0:T(1024)} %get-tuple-element.53) | copy-start | bytes 18436
  211.9 75.7 %copy-start.17 = (f32[1536]{0:T(1024)S(1)}, f32[1536]{0:T(1024)}, u32[]{:S(2)}) copy-start(f32[1536]{0:T(1024)} %get-tuple-element.54) | copy-start | bytes 18436
  211.9 75.7 %copy-start.18 = (f32[1536]{0:T(1024)S(1)}, f32[1536]{0:T(1024)}, u32[]{:S(2)}) copy-start(f32[1536]{0:T(1024)} %get-tuple-element.55) | copy-start | bytes 18436
  211.9 75.7 %copy-start.19 = (f32[1536]{0:T(1024)S(1)}, f32[1536]{0:T(1024)}, u32[]{:S(2)}) copy-start(f32[1536]{0:T(1024)} %get-tuple-element.56) | copy-start | bytes 18436
  211.9 75.7 %copy-start.20 = (f32[1536]{0:T(1024)S(1)}, f32[1536]{0:T(1024)}, u32[]{:S(2)}) copy-start(f32[1536]{0:T(1024)} %get-tuple-element.57) | copy-start | bytes 18436
  211.9 75.7 %copy-start.21 = (f32[1536]{0:T(1024)S(1)}, f32[1536]{0:T(1024)}, u32[]{:S(2)}) copy-start(f32[1536]{0:T(1024)} %get-tuple-element.58) | copy-start | bytes 18436
  211.9 75.7 %copy-start.22 = (f32[1536]{0:T(1024)S(1)}, f32[1536]{0:T(1024)}, u32[]{:S(2)}) copy-start(f32[1536]{0:T(1024)} %get-tuple-element.59) | copy-start | bytes 18436
  211.9 75.7 %copy-start.24 = (f32[1536]{0:T(1024)S(1)}, f32[1536]{0:T(1024)}, u32[]{:S(2)}) copy-start(f32[1536]{0:T(1024)} %copy-done.23) | copy-start | bytes 18436
  (50 other events, 1364.2 us)
Sparse Core Ops, SparseCore 0:
  286.2 161.5 all-reduce.3
where the time goes:
time: 460 us
  other arithmetic  258 us (56%)
  blocking collectives  68.1 us (15%)
  waiting for transfers between devices  45 us (10%)
  local copies, waits for them, and re-layouts  33.7 us (7%)
  matrix products  27.3 us (6%)
  between operations  15.2 us (3%)
  starting transfers between devices  11.9 us (3%)
    convert_element_type x1, other arithmetic, local(): grad_input = grad_lane.astype(jnp.bfloat16)  115 us
    reduce_sum x1, other arithmetic, local(): average = jnp.mean(conv, axis=-1, keepdims=True)  81.3 us
    psum x1, blocking collectives, local(): lax.psum((local_kernel, local_gain, local_bias), ('dp', 'seq'))  68.1 us
    reduce_sum x5, other arithmetic, local(): jnp.sum(grad_conv * padded[:, offset:offset + slab_rows].astype(jnp.float...  48.1 us
    psum x1, waiting for transfers between devices, local(): summed_outer = lax.psum(local_outer, ('dp', 'seq'))  45 us
    another operation x32, local copies, waits for them, and re-layouts, local(): local_kernel = jnp.stack(kernel_rows, axis=0)  24.4 us
    dot_general x1, matrix products, local(): lax.dot_general(cot_rows, w_out, (((1,), (1,)), ((), ())), preferred_elem...  13.2 us
    ppermute x2, starting transfers between devices, padded_2(): before = lax.ppermute(last, axis, up)  9.33 us
  transfers between devices with their start and end apart: 5, of which 1 were waited for; matrix products, arithmetic and copies ran while one was open for 32% of the time, Pallas kernels for 0%

commit v1 on v0

v1 whole, which is shorter than its diff:
```python
import functools
import math

import jax
import jax.numpy as jnp
import numpy as np
from jax import lax
from jax.experimental import pallas as pl
from jax.experimental.pallas import tpu as pltpu
from jax.sharding import PartitionSpec as P

EPSILON = 1e-05
TAPS = 31
HALF = TAPS // 2
ROWS = 128
EDGE = 16
WINDOW = ROWS + 2 * EDGE
POINTS = 256
BINS = POINTS // 2
f32, bf16 = jnp.float32, jnp.bfloat16


def tables():
    place = np.arange(POINTS)
    bins = np.arange(BINS)[:, None]
    cosines = math.sqrt(2.0 / POINTS) * np.cos(2 * np.pi * ((bins * place) % POINTS) / POINTS)
    sines = math.sqrt(2.0 / POINTS) * np.sin(2 * np.pi * ((bins * place) % POINTS) / POINTS)
    cosines[0] = 1.0 / math.sqrt(POINTS)
    sines[0] = (1.0 - 2.0 * (place % 2)) / math.sqrt(POINTS)
    basis = np.concatenate([cosines, sines])
    high = basis.astype(jnp.bfloat16)
    low = (basis - high.astype(np.float64)).astype(jnp.bfloat16)
    split = np.concatenate([high, low])
    lags = np.arange(TAPS) - HALF
    turn = 2 * np.pi * ((bins * lags) % POINTS) / POINTS
    real, imag = np.cos(turn), np.sin(turn)
    other = real.copy()
    other[0] = 1.0 - 2.0 * (np.abs(lags) % 2)
    spectrum = np.concatenate([real, imag, other]).astype(np.float32)
    gather = np.concatenate([real, other, -imag]).astype(np.float32)
    return split, spectrum, gather


def gapped(lengths_ref, lane, first, shape, dim, skip):
    row = lax.broadcasted_iota(jnp.int32, shape, dim) + skip
    frame = first + row
    place, end = row, 0
    for utter in range(lengths_ref.shape[1] - 1):
        end = end + lengths_ref[lane, utter]
        place = place + jnp.where(frame >= end, jnp.where(first < end, HALF, 0), 0)
    return place


def chosen_columns(split, place):
    count = place.shape[1]
    one_hot = (lax.broadcasted_iota(jnp.int32, (POINTS, count), 0) == place).astype(f32).astype(bf16)
    return jnp.dot(split, one_hot, preferred_element_type=f32).astype(bf16)


def chosen_rows(split_t, place):
    count = place.shape[0]
    one_hot = (lax.broadcasted_iota(jnp.int32, (count, POINTS), 1) == place).astype(f32).astype(bf16)
    return jnp.dot(one_hot, split_t, preferred_element_type=f32).astype(bf16)


def dot(a, b):
    return jnp.dot(a, b, preferred_element_type=f32)


def sigmoid(a):
    return 0.5 * jnp.tanh(0.5 * a) + 0.5


def forward_kernel(blocks, meta_ref, lengths_ref, x_ref, prev_ref, next_ref, before_ref, after_ref, split_ref,
                   split_t_ref, spec_ref, gain_ref, bias_ref, sw_ref, normed_ref, istd_ref, xhat_ref, win, conv):
    step = pl.program_id(0)
    lane, block = step // blocks, step % blocks
    channels = x_ref.shape[1]
    first = meta_ref[0] + block * ROWS - EDGE
    win[EDGE : EDGE + ROWS] = x_ref[...]
    win[:EDGE] = jnp.where(block == 0, before_ref[...], prev_ref[...])
    win[EDGE + ROWS :] = jnp.where(block == blocks - 1, after_ref[...], next_ref[...])
    into = chosen_columns(split_ref[...], gapped(lengths_ref, lane, first, (1, WINDOW), 1, 0))
    back = chosen_rows(split_t_ref[...], gapped(lengths_ref, lane, first, (ROWS, 1), 0, EDGE))
    width = 512
    for at in range(0, channels, width):
        cols = slice(at, at + width)
        rows = win[:, cols]
        xhat = dot(into[:POINTS], rows) + dot(into[POINTS:], rows)
        xhat_ref[:, cols] = xhat.astype(bf16)
        real, imag = xhat[:BINS], xhat[BINS:]
        p, q, other = spec_ref[:BINS, cols], spec_ref[BINS:POINTS, cols], spec_ref[POINTS:, cols]
        zed = jnp.concatenate([real * p + imag * q, imag * other - real * q]).astype(bf16)
        conv[:, cols] = dot(back[:, :POINTS], zed) + dot(back[:, POINTS:], zed)
    gain, bias = gain_ref[...], bias_ref[...]
    strip = 16
    for at in range(0, ROWS, strip):
        rows = slice(at, at + strip)
        value = conv[rows]
        centred = value - jnp.sum(value, axis=1, keepdims=True) * (1.0 / channels)
        variance = jnp.sum(centred * centred, axis=1, keepdims=True) * (1.0 / channels)
        inv_std = lax.rsqrt(variance + EPSILON)
        normed = centred * inv_std
        affine = normed * gain + bias
        sw_ref[rows] = (affine * sigmoid(affine)).astype(bf16)
        normed_ref[rows] = normed
        istd_ref[rows] = jnp.broadcast_to(inv_std, (strip, istd_ref.shape[1]))


def backward_kernel(blocks, meta_ref, lengths_ref, cot_ref, sw_ref, normed_ref, istd_ref, xhat_ref, w_ref, split_ref,
                    split_t_ref, spec_ref, gather_ref, gain_ref, bias_ref, layer_ref, gi_ref, edge_ref, small_ref,
                    gs, g, acc, sums, pending, tail):
    step = pl.program_id(0)
    lane, block = step // blocks, step % blocks
    channels = cot_ref.shape[1]
    first = meta_ref[0] + block * ROWS - EDGE

    @pl.when(step == 0)
    def _():
        acc[...] = jnp.zeros_like(acc)
        sums[...] = jnp.zeros_like(sums)

    layer_ref[...] = dot(sw_ref[...], w_ref[...]).astype(bf16)
    gs[...] = lax.dot_general(cot_ref[...], w_ref[...], (((1,), (1,)), ((), ())), preferred_element_type=f32)
    gain, bias = gain_ref[...], bias_ref[...]
    strip = 16
    for at in range(0, ROWS, strip):
        rows = slice(at, at + strip)
        normed = normed_ref[rows]
        affine = normed * gain + bias
        gate = sigmoid(affine)
        grad = gs[rows] * gate * (1.0 + affine * (1.0 - gate))
        prod = grad * normed
        sums[:8] += prod[:8] + prod[8:]
        sums[8:] += grad[:8] + grad[8:]
        grad_normed = grad * gain
        mean = jnp.sum(grad_normed, axis=1, keepdims=True) * (1.0 / channels)
        along = jnp.sum(grad_normed * normed, axis=1, keepdims=True) * (1.0 / channels)
        out = (istd_ref[rows, :1] * (grad_normed - mean - normed * along)).astype(bf16)
        g[rows] = out
        g[ROWS + at : ROWS + at + strip] = out
    into = chosen_columns(split_ref[...], gapped(lengths_ref, lane, first, (1, ROWS), 1, EDGE))
    into = jnp.concatenate([into[:POINTS], into[POINTS:]], axis=1)
    back = chosen_rows(split_t_ref[...], gapped(lengths_ref, lane, first, (WINDOW, 1), 0, 0))
    is_first, is_last = block == 0, block == blocks - 1
    base = pl.multiple_of(step * ROWS, ROWS)
    width = 512
    for at in range(0, channels, width):
        cols = slice(at, at + width)
        ghat = dot(into, g[:, cols])
        cg, sg = ghat[:BINS], ghat[BINS:]
        cx, sx = xhat_ref[:BINS, cols].astype(f32), xhat_ref[BINS:, cols].astype(f32)
        acc[:BINS, cols] += cg * cx
        acc[BINS:POINTS, cols] += sg * sx
        acc[POINTS:, cols] += sg * cx - cg * sx
        p, q, other = spec_ref[:BINS, cols], spec_ref[BINS:POINTS, cols], spec_ref[POINTS:, cols]
        vee = jnp.concatenate([cg * p - sg * q, sg * other + cg * q]).astype(bf16)
        part = dot(back[:, :POINTS], vee) + dot(back[:, POINTS:], vee)
        own = part[EDGE : EDGE + ROWS]
        carried = jnp.where(is_first, 0.0, tail[:, cols])
        gi_ref[pl.ds(base, EDGE), cols] = (own[:EDGE] + carried).astype(bf16)
        gi_ref[pl.ds(base + EDGE, ROWS - 2 * EDGE), cols] = own[EDGE : ROWS - EDGE].astype(bf16)
        gi_ref[pl.ds(base + ROWS - EDGE, EDGE), cols] = own[ROWS - EDGE :].astype(bf16)
        head = part[:EDGE]

        @pl.when(jnp.logical_not(is_first))
        def _():
            gi_ref[pl.ds(pl.multiple_of(base - EDGE, EDGE), EDGE), cols] = (pending[:, cols] + head).astype(bf16)

        @pl.when(is_first)
        def _():
            edge_ref[pl.ds(lane * 2 * EDGE, EDGE), cols] = head.astype(bf16)

        pending[:, cols] = own[ROWS - EDGE :]
        tail[:, cols] = part[EDGE + ROWS :]

        @pl.when(is_last)
        def _():
            edge_ref[pl.ds(lane * 2 * EDGE + EDGE, EDGE), cols] = part[EDGE + ROWS :].astype(bf16)

    @pl.when(step == pl.num_programs(0) - 1)
    def _():
        table = gather_ref[...]
        table_high = table.astype(bf16)
        table_low = (table - table_high.astype(f32)).astype(bf16)
        for at in range(0, channels, width):
            cols = slice(at, at + width)
            value = acc[:, cols]
            high = value.astype(bf16)
            low = (value - high.astype(f32)).astype(bf16)
            small_ref[:32, cols] = dot(table_high, high) + dot(table_low, high) + dot(table_high, low)
        prod, grad = sums[:8], sums[8:]
        small_ref[32:40] = jnp.concatenate(
            [
                jnp.sum(prod, axis=0, keepdims=True),
                jnp.sum(grad, axis=0, keepdims=True),
                jnp.zeros((6, channels), f32),
            ]
        )


def whole(shape):
    return pl.BlockSpec(shape, lambda i: (0,) * len(shape))


SMEM = pl.BlockSpec(memory_space=pltpu.SMEM)


def forward(meta, lengths, x, before, after, split, split_t, spec, gain, bias, interpret=False):
    lanes, length, channels = x.shape
    blocks = length // ROWS
    steps = lanes * blocks
    flat = x.reshape(lanes * length, channels)
    per = ROWS // EDGE
    last = lanes * length // EDGE - 1
    row = pl.BlockSpec((ROWS, channels), lambda i: (i, 0))
    halo = pl.BlockSpec((EDGE, channels), lambda i: (i // blocks, 0))
    return pl.pallas_call(
        functools.partial(forward_kernel, blocks),
        grid=(steps,),
        in_specs=[
            SMEM,
            SMEM,
            row,
            pl.BlockSpec((EDGE, channels), lambda i: (jnp.maximum(i * per - 1, 0), 0)),
            pl.BlockSpec((EDGE, channels), lambda i: (jnp.minimum(i * per + per, last), 0)),
            halo,
            halo,
            whole(split.shape),
            whole(split_t.shape),
            whole(spec.shape),
            whole((1, channels)),
            whole((1, channels)),
        ],
        out_specs=[
            row,
            row,
            pl.BlockSpec((ROWS, 128), lambda i: (i, 0)),
            pl.BlockSpec((POINTS, channels), lambda i: (i, 0)),
        ],
        out_shape=[
            jax.ShapeDtypeStruct((lanes * length, channels), bf16),
            jax.ShapeDtypeStruct((lanes * length, channels), f32),
            jax.ShapeDtypeStruct((lanes * length, 128), f32),
            jax.ShapeDtypeStruct((steps * POINTS, channels), bf16),
        ],
        scratch_shapes=[pltpu.VMEM((WINDOW, channels), bf16), pltpu.VMEM((ROWS, channels), f32)],
        compiler_params=pltpu.CompilerParams(vmem_limit_bytes=40 << 20),
        interpret=interpret,
        name="conv_norm_swish",
    )(
        meta,
        lengths,
        flat,
        flat,
        flat,
        before.reshape(lanes * EDGE, channels),
        after.reshape(lanes * EDGE, channels),
        split,
        split_t,
        spec,
        gain,
        bias,
    )


def backward(meta, lengths, cot, sw, normed, istd, xhat, w, split, split_t, spec, gather, gain, bias, lanes,
             interpret=False):
    total, channels = cot.shape
    steps = total // ROWS
    blocks = steps // lanes
    row = pl.BlockSpec((ROWS, channels), lambda i: (i, 0))
    return pl.pallas_call(
        functools.partial(backward_kernel, blocks),
        grid=(steps,),
        in_specs=[
            SMEM,
            SMEM,
            row,
            row,
            row,
            pl.BlockSpec((ROWS, 128), lambda i: (i, 0)),
            pl.BlockSpec((POINTS, channels), lambda i: (i, 0)),
            whole(w.shape),
            whole(split.shape),
            whole(split_t.shape),
            whole(spec.shape),
            whole(gather.shape),
            whole((1, channels)),
            whole((1, channels)),
        ],
        out_specs=[row, whole((total, channels)), whole((lanes * 2 * EDGE, channels)), whole((40, channels))],
        out_shape=[
            jax.ShapeDtypeStruct((total, channels), bf16),
            jax.ShapeDtypeStruct((total, channels), bf16),
            jax.ShapeDtypeStruct((lanes * 2 * EDGE, channels), bf16),
            jax.ShapeDtypeStruct((40, channels), f32),
        ],
        scratch_shapes=[
            pltpu.VMEM((ROWS, channels), f32),
            pltpu.VMEM((2 * ROWS, channels), bf16),
            pltpu.VMEM((3 * BINS, channels), f32),
            pltpu.VMEM((16, channels), f32),
            pltpu.VMEM((EDGE, channels), f32),
            pltpu.VMEM((EDGE, channels), f32),
        ],
        compiler_params=pltpu.CompilerParams(vmem_limit_bytes=56 << 20),
        interpret=interpret,
        name="backward",
    )(meta, lengths, cot, sw, normed, istd, xhat, w, split, split_t, spec, gather, gain, bias)


def shifts(size):
    up = [(i, i + 1) for i in range(size - 1)]
    return up, [(j, i) for i, j in up]


def local(glu_out, lengths, kernel, norm_gain, norm_bias, w_out, cotangent, interpret=False):
    lanes, length, channels = glu_out.shape
    seq_count = lax.axis_size("seq")
    norm_scale = 1.0 / math.sqrt(lanes * lax.axis_size("dp") * length * seq_count)
    seq_place = lax.axis_index("seq")
    up, down = shifts(seq_count)
    before = lax.ppermute(glu_out[:, length - EDGE :], "seq", up)
    after = lax.ppermute(glu_out[:, :EDGE], "seq", down)
    split, spectrum, gather = tables()
    spec = jnp.dot(jnp.asarray(spectrum), kernel, precision=lax.Precision.HIGHEST)
    split_t = jnp.asarray(np.ascontiguousarray(split.T))
    split = jnp.asarray(split)
    table = np.zeros((32, 3 * BINS), np.float32)
    table[:TAPS] = gather.T
    gain, bias = norm_gain.reshape(1, channels), norm_bias.reshape(1, channels)
    meta = jnp.reshape(seq_place * length, (1,)).astype(jnp.int32)
    sw, normed, istd, xhat = forward(
        meta, lengths, glu_out, before, after, split, split_t, spec, gain, bias, interpret=interpret
    )
    cot = cotangent.reshape(-1, channels)
    outer = lax.dot_general(sw, cot, (((0,), (0,)), ((), ())), preferred_element_type=f32)
    summed = lax.psum(outer, ("dp", "seq"))
    share = channels // seq_count
    grad_w = lax.dynamic_slice_in_dim(summed, seq_place * share, share, 0) * norm_scale
    layer, gi, edge, small = backward(
        meta, lengths, cot, sw, normed, istd, xhat, w_out, split, split_t, spec, jnp.asarray(table), gain, bias, lanes,
        interpret=interpret,
    )
    edge = edge.reshape(lanes, 2, EDGE, channels)
    from_after = lax.ppermute(edge[:, 0], "seq", down)
    from_before = lax.ppermute(edge[:, 1], "seq", up)
    gi = gi.reshape(lanes, length, channels)
    gi = gi.at[:, :EDGE].add(from_before).at[:, length - EDGE :].add(from_after)
    small = lax.psum(small, ("dp", "seq")) * norm_scale
    return (
        layer.reshape(lanes, length, channels),
        gi,
        grad_w,
        small[:TAPS],
        small[32],
        small[33],
    )


def solution(mesh):
    in_specs = (P("dp", "seq", None), P("dp", None), P(), P(), P(), P(), P("dp", "seq", None))
    out_specs = (P("dp", "seq", None), P("dp", "seq", None), P("seq", None), P(), P(), P())
    return jax.shard_map(local, mesh=mesh, in_specs=in_specs, out_specs=out_specs, check_vma=False)
```

time: 460 us -> 272 us (0.59)
  other arithmetic: 258 us -> 7.37 us
  waiting for transfers between devices: 45 us -> 159 us
  blocking collectives: 68.1 us -> 0 us
  Pallas kernels: 0 us -> 59.4 us
  local copies, waits for them, and re-layouts: 33.7 us -> 9 us
  matrix products: 27.3 us -> 12 us
    reduce_sum x8 -> x0, other arithmetic: 133 us -> none  [the longest x1 81.3 us: local(): average = jnp.mean(conv, axis=-1, keepdims=True)]
    convert_element_type x5 -> x0, other arithmetic: 118 us -> none  [the longest x1 115 us: local(): grad_input = grad_lane.astype(jnp.bfloat16)]
    psum x1, waiting for transfers between devices: 45 us -> 156 us  [local(): summed = lax.psum(outer, ('dp', 'seq'))]
    psum x1 -> x0, blocking collectives: 68.1 us -> none  [local(): lax.psum((local_kernel, local_gain, local_bias), ('dp', 'seq'))]
    pallas_call x0 -> x2, Pallas kernels: none -> 59.4 us  [the longest x1 42.6 us: backward(): pl.pallas_call(functools.partial(backward_kernel, blocks), grid=(steps,),...]
    another operation x32 -> x0, local copies, waits for them, and re-layouts: 24.4 us -> none  [local(): local_kernel = jnp.stack(kernel_rows, axis=0)]
    dot_general x3 -> x2, matrix products: 27.3 us -> 12 us  [the longest x1 7.71 us: local(): lax.dot_general(sw, cot, (((0,), (0,)), ((), ())), preferred_element_type...]
  transfers between devices with their start and end apart: 5 -> 5, of which waited for: 1 -> 3; matrix products, arithmetic and copies ran while one was open for 32% -> 3% of each run, Pallas kernels for 0% -> 0%
where the time goes in v1:
time: 272 us; the launch traced here: 271 us
  waiting for transfers between devices  159 us (58%)
  Pallas kernels  59.4 us (22%)
  between operations  14.2 us (5%)
  matrix products  12 us (4%)
  starting transfers between devices  10.6 us (4%)
  local copies, waits for them, and re-layouts  9 us (3%)
  other arithmetic  7.37 us (3%)
    psum x1, waiting for transfers between devices, local(): summed = lax.psum(outer, ('dp', 'seq'))  156 us
    pallas_call x1, Pallas kernels, backward(): pl.pallas_call(functools.partial(backward_kernel, blocks), grid=(steps,),...  42.6 us
    pallas_call x1, Pallas kernels, forward(): pl.pallas_call(functools.partial(forward_kernel, blocks), grid=(steps,),...  16.8 us
    dot_general x1, matrix products, local(): lax.dot_general(sw, cot, (((0,), (0,)), ((), ())), preferred_element_type...  7.71 us
  transfers between devices with their start and end apart: 5, of which 3 were waited for; matrix products, arithmetic and copies ran while one was open for 3% of the time, Pallas kernels for 0%

profile of v1, /device:TPU:1, one launch (start us, length us, event | category | flops | bytes accessed | tf_op | source)
XLA Modules:
  0.0 271.5 jit_solution(17775736618235591448)
XLA Ops:
  7.2 0.0 copy-start
  7.2 0.0 all-reduce.3.cloned.1.call-start
  7.2 1.8 fusion.2
  9.0 1.3 collective-permute-start.1
  10.3 4.7 %collective-permute-start = (bf16[2,16,1536]{2,1,0:T(8,128)(2,1)}, bf16[2,16,1536]{2,1,0:T(8,128)(2,1)S(1)}, u32[]{:S(2)}, u32[]{:S(2)}) collective-permute-start(bf16[2,16,1536]{2,1,0:T(8,128)(2,1)} %get-tuple-element.51), channel_id=1, source_target_pairs={{0,1},{1,2},{2,3},{4,5},{5,6},{6,7},{8,9},{9,10},{10,11},{12,13},{... | collective-permute-start | bytes 294920 | tf_op jit(solution)/shard_map/ppermute | solution.py:324
  15.0 4.3 %fusion.3.spec_ref = f32[384,1536]{1,0:T(8,128)} fusion(f32[384,31]{1,0:T(8,128)} %constant.77.clone, f32[31,1536]{1,0:T(8,128)S(1)} %copy-done), kind=kOutput, calls=%fused_computation.11 | convolution fusion | flops 219414528 | bytes 2597376 | tf_op jit(solution)/shard_map/dot_general | solution.py:327
  19.3 0.0 copy-start.7
  19.3 0.7 reshape.108.bias_ref
  20.0 0.0 collective-permute-done.1
  20.1 0.0 collective-permute-done
  20.1 0.0 copy-start.2
  20.1 1.7 copy-done.2
  21.7 0.9 copy-done.4
  22.7 0.9 copy-done.5
  23.6 0.7 copy-done.9
  24.3 16.8 %conv_norm_swish.1 = (bf16[1024,1536]{1,0:T(8,128)(2,1)S(1)}, f32[1024,1536]{1,0:T(8,128)}, f32[1024,128]{1,0:T(8,128)S(1)}, bf16[2048,1536]{1,0:T(8,128)(2,1)}) custom-call(s32[1]{0:T(128)} %bitcast.meta_ref, s32[2,8]{1,0:T(2,128)S(1)} %copy-done.9, bf16[1024,1536]{1,0:T(8,128)(2,1)S(1)} %bitcast.20, bf16[1024,1536]{1,0:T(8,128)(2,1)S(1)} %bitcast.21, ...), custom_call_target="tpu_custom_call" | custom-call | tf_op jit(solution)/shard_map/conv_norm_swish/pallas_call | solution.py:218
  41.2 7.7 %fusion.4 = f32[1536,1536]{1,0:T(8,128)} fusion(bf16[1024,1536]{1,0:T(8,128)(2,1)S(1)} %get-tuple-element.38.sw_ref, bf16[1024,1536]{1,0:T(8,128)(2,1)S(1)} %bitcast.26), kind=kOutput, calls=%fused_computation.12 | convolution fusion | flops 4831838208 | bytes 15728640 | tf_op jit(solution)/shard_map/dot_general | solution.py:338
  48.9 42.6 %backward.1 = (bf16[1024,1536]{1,0:T(8,128)(2,1)}, bf16[1024,1536]{1,0:T(8,128)(2,1)}, bf16[64,1536]{1,0:T(8,128)(2,1)}, f32[40,1536]{1,0:T(8,128)}) custom-call(s32[1]{0:T(128)} %bitcast.meta_ref, s32[2,8]{1,0:T(2,128)} %lengths_ref.3, bf16[1024,1536]{1,0:T(8,128)(2,1)} %bitcast.25, bf16[1024,1536]{1,0:T(8,128)(2,1)} %copy-done.3, ...), custom_call_target="tpu_custom_call" | custom-call | tf_op jit(solution)/shard_map/backward/pallas_call | solution.py:273
  91.5 0.0 copy-start.11
  91.5 0.0 all-reduce.3.cloned.1.call-update
  91.5 0.9 copy-done.11
  92.5 3.4 %collective-permute-start.2 = (bf16[2,16,1536]{2,1,0:T(8,128)(2,1)S(1)}, bf16[2,16,1536]{2,1,0:T(8,128)(2,1)S(1)}, u32[]{:S(2)}, u32[]{:S(2)}) collective-permute-start(bf16[2,16,1536]{2,1,0:T(8,128)(2,1)S(1)} %get-tuple-element.53), channel_id=1, source_target_pairs={{0,1},{1,2},{2,3},{4,5},{5,6},{6,7},{8,9},{9,10},{10,11},{12,13},{... | collective-permute-start | bytes 294920 | tf_op jit(solution)/shard_map/ppermute | solution.py:348
  95.8 1.3 collective-permute-start.3
  97.1 0.3 collective-permute-done.2
  97.4 1.6 fusion.1
  99.0 2.2 collective-permute-done.3
  101.2 1.6 fusion
  102.7 156.3 %all-reduce.3.cloned.1.call-done = (f32[1536,1536]{1,0:T(8,128)}, f32[40,1536]{1,0:T(8,128)}) async-done(((f32[1536,1536]{1,0:T(8,128)}, f32[40,1536]{1,0:T(8,128)}), (f32[1536,1536]{1,0:T(8,128)}, f32[40,1536]{1,0:T(8,128)})) %all-reduce.3.cloned.1.call-update) | async-done | bytes 9682960 | tf_op jit(solution)/shard_map/psum | solution.py:339
  259.1 1.0 broadcast_multiply_fusion
  260.0 0.6 slice_reduce_fusion
  260.7 0.7 slice.82
  261.4 3.3 %dynamic-slice_multiply_fusion = f32[384,1536]{1,0:T(8,128)} fusion(f32[1536,1536]{1,0:T(8,128)} %get-tuple-element.48, s32[]{:T(128)S(6)} %select_n.3), kind=kLoop, calls=%fused_computation | loop fusion | flops 589824 | bytes 4718596 | tf_op jit(solution)/shard_map/mul | solution.py:341
  (19 shorter events, 0.1 us)
Async XLA Ops:
  7.2 7.8 %copy-start = (f32[31,1536]{1,0:T(8,128)S(1)}, f32[31,1536]{1,0:T(8,128)}, u32[]{:S(2)}) copy-start(f32[31,1536]{1,0:T(8,128)} %param.17) | copy-start | bytes 571396
  7.2 12.9 %copy-start.1 = (bf16[2,512,1536]{2,1,0:T(8,128)(2,1)S(1)}, bf16[2,512,1536]{2,1,0:T(8,128)(2,1)}, u32[]{:S(2)}) copy-start(bf16[2,512,1536]{2,1,0:T(8,128)(2,1)} %param.15) | copy-start | bytes 9437188
  7.2 12.1 %copy-start.12 = (f32[1536]{0:T(1024)S(1)}, f32[1536]{0:T(1024)}, u32[]{:S(2)}) copy-start(f32[1536]{0:T(1024)} %param.18) | copy-start | bytes 18436
  7.2 251.9 %all-reduce.3.cloned.1.call-start = ((), (), s32[]{:S(2)}) async-start(), calls=%async_computation | async-start | bytes 19365888 | tf_op jit(solution)/shard_map/psum | solution.py:339
  9.0 11.0 %collective-permute-start.1 = (bf16[2,16,1536]{2,1,0:T(8,128)(2,1)}, bf16[2,16,1536]{2,1,0:T(8,128)(2,1)S(1)}, u32[]{:S(2)}, u32[]{:S(2)}) collective-permute-start(bf16[2,16,1536]{2,1,0:T(8,128)(2,1)} %get-tuple-element.50), channel_id=1, source_target_pairs={{1,0},{2,1},{3,2},{5,4},{6,5},{7,6},{9,8},{10,9},{11,10},{13,12},{... | collective-permute-start | bytes 294920 | tf_op jit(solution)/shard_map/ppermute | solution.py:325
  10.3 9.7 %collective-permute-start = (bf16[2,16,1536]{2,1,0:T(8,128)(2,1)}, bf16[2,16,1536]{2,1,0:T(8,128)(2,1)S(1)}, u32[]{:S(2)}, u32[]{:S(2)}) collective-permute-start(bf16[2,16,1536]{2,1,0:T(8,128)(2,1)} %get-tuple-element.51), channel_id=1, source_target_pairs={{0,1},{1,2},{2,3},{4,5},{5,6},{6,7},{8,9},{9,10},{10,11},{12,13},{... | collective-permute-start | bytes 294920 | tf_op jit(solution)/shard_map/ppermute | solution.py:324
  19.3 21.8 %copy-start.7 = (f32[1,1536]{1,0:T(1,128)}, f32[1,1536]{1,0:T(1,128)S(1)}, u32[]{:S(2)}) copy-start(f32[1,1536]{1,0:T(1,128)S(1)} %reshape.107.gain_ref) | copy-start | bytes 18436
  20.0 21.1 %copy-start.8 = (f32[1,1536]{1,0:T(1,128)}, f32[1,1536]{1,0:T(1,128)S(1)}, u32[]{:S(2)}) copy-start(f32[1,1536]{1,0:T(1,128)S(1)} %reshape.108.bias_ref) | copy-start | bytes 18436
  20.1 1.7 copy-start.2
  21.7 0.9 copy-start.4
  22.7 0.9 copy-start.5
  23.6 0.7 copy-start.9
  24.3 16.9 %copy-start.10 = (bf16[2,512,1536]{2,1,0:T(8,128)(2,1)S(1)}, bf16[2,512,1536]{2,1,0:T(8,128)(2,1)}, u32[]{:S(2)}) copy-start(bf16[2,512,1536]{2,1,0:T(8,128)(2,1)} %param.21) | copy-start | bytes 9437188
  41.2 7.7 %copy-start.3 = (bf16[1024,1536]{1,0:T(8,128)(2,1)}, bf16[1024,1536]{1,0:T(8,128)(2,1)S(1)}, u32[]{:S(2)}) copy-start(bf16[1024,1536]{1,0:T(8,128)(2,1)S(1)} %get-tuple-element.38.sw_ref) | copy-start | bytes 9437188
  41.2 7.7 %copy-start.6 = (f32[1024,128]{1,0:T(8,128)}, f32[1024,128]{1,0:T(8,128)S(1)}, u32[]{:S(2)}) copy-start(f32[1024,128]{1,0:T(8,128)S(1)} %get-tuple-element.40.istd_ref) | copy-start | bytes 1572868
  91.5 0.9 copy-start.11
  92.5 5.0 %collective-permute-start.2 = (bf16[2,16,1536]{2,1,0:T(8,128)(2,1)S(1)}, bf16[2,16,1536]{2,1,0:T(8,128)(2,1)S(1)}, u32[]{:S(2)}, u32[]{:S(2)}) collective-permute-start(bf16[2,16,1536]{2,1,0:T(8,128)(2,1)S(1)} %get-tuple-element.53), channel_id=1, source_target_pairs={{0,1},{1,2},{2,3},{4,5},{5,6},{6,7},{8,9},{9,10},{10,11},{12,13},{... | collective-permute-start | bytes 294920 | tf_op jit(solution)/shard_map/ppermute | solution.py:348
  95.8 5.4 %collective-permute-start.3 = (bf16[2,16,1536]{2,1,0:T(8,128)(2,1)S(1)}, bf16[2,16,1536]{2,1,0:T(8,128)(2,1)S(1)}, u32[]{:S(2)}, u32[]{:S(2)}) collective-permute-start(bf16[2,16,1536]{2,1,0:T(8,128)(2,1)S(1)} %get-tuple-element.52), channel_id=1, source_target_pairs={{1,0},{2,1},{3,2},{5,4},{6,5},{7,6},{9,8},{10,9},{11,10},{13,12},{... | collective-permute-start | bytes 294920 | tf_op jit(solution)/shard_map/ppermute | solution.py:347
Sparse Core Ops, SparseCore 0:
  91.7 167.3 all-reduce.2

commit v2 on v1

--- a/solution.py
+++ b/solution.py
@@ -38,7 +38,9 @@
     other[0] = 1.0 - 2.0 * (np.abs(lags) % 2)
     spectrum = np.concatenate([real, imag, other]).astype(np.float32)
     gather = np.concatenate([real, other, -imag]).astype(np.float32)
-    return split, spectrum, gather
+    wide, deep = np.zeros((3 * BINS, 32), np.float32), np.zeros((32, 3 * BINS), np.float32)
+    wide[:, :TAPS], deep[:TAPS] = spectrum, gather.T
+    return split, np.ascontiguousarray(split.T), wide, deep
 
 
 def gapped(lengths_ref, lane, first, shape, dim, skip):
@@ -71,10 +73,9 @@
     return 0.5 * jnp.tanh(0.5 * a) + 0.5
 
 
-def forward_kernel(blocks, meta_ref, lengths_ref, x_ref, prev_ref, next_ref, before_ref, after_ref, split_ref,
+def forward_kernel(lane, blocks, meta_ref, lengths_ref, x_ref, prev_ref, next_ref, before_ref, after_ref, split_ref,
                    split_t_ref, spec_ref, gain_ref, bias_ref, sw_ref, normed_ref, istd_ref, xhat_ref, win, conv):
-    step = pl.program_id(0)
-    lane, block = step // blocks, step % blocks
+    block = pl.program_id(0)
     channels = x_ref.shape[1]
     first = meta_ref[0] + block * ROWS - EDGE
     win[EDGE : EDGE + ROWS] = x_ref[...]
@@ -107,15 +108,14 @@
         istd_ref[rows] = jnp.broadcast_to(inv_std, (strip, istd_ref.shape[1]))
 
 
-def backward_kernel(blocks, meta_ref, lengths_ref, cot_ref, sw_ref, normed_ref, istd_ref, xhat_ref, w_ref, split_ref,
+def backward_kernel(lane, blocks, meta_ref, lengths_ref, cot_ref, sw_ref, normed_ref, istd_ref, xhat_ref, w_ref, split_ref,
                     split_t_ref, spec_ref, gather_ref, gain_ref, bias_ref, layer_ref, gi_ref, edge_ref, small_ref,
                     gs, g, acc, sums, pending, tail):
-    step = pl.program_id(0)
-    lane, block = step // blocks, step % blocks
+    block = pl.program_id(0)
     channels = cot_ref.shape[1]
     first = meta_ref[0] + block * ROWS - EDGE
 
-    @pl.when(step == 0)
+    @pl.when(block == 0)
     def _():
         acc[...] = jnp.zeros_like(acc)
         sums[...] = jnp.zeros_like(sums)
@@ -143,7 +143,7 @@
     into = jnp.concatenate([into[:POINTS], into[POINTS:]], axis=1)
     back = chosen_rows(split_t_ref[...], gapped(lengths_ref, lane, first, (WINDOW, 1), 0, 0))
     is_first, is_last = block == 0, block == blocks - 1
-    base = pl.multiple_of(step * ROWS, ROWS)
+    base = pl.multiple_of(block * ROWS, ROWS)
     width = 512
     for at in range(0, channels, width):
         cols = slice(at, at + width)
@@ -169,16 +169,16 @@
 
         @pl.when(is_first)
         def _():
-            edge_ref[pl.ds(lane * 2 * EDGE, EDGE), cols] = head.astype(bf16)
+            edge_ref[:EDGE, cols] = head.astype(bf16)
 
         pending[:, cols] = own[ROWS - EDGE :]
         tail[:, cols] = part[EDGE + ROWS :]
 
         @pl.when(is_last)
         def _():
-            edge_ref[pl.ds(lane * 2 * EDGE + EDGE, EDGE), cols] = part[EDGE + ROWS :].astype(bf16)
-
-    @pl.when(step == pl.num_programs(0) - 1)
+            edge_ref[EDGE:, cols] = part[EDGE + ROWS :].astype(bf16)
+
+    @pl.when(is_last)
     def _():
         table = gather_ref[...]
         table_high = table.astype(bf16)
@@ -199,31 +199,100 @@
         )
 
 
+def halves(value):
+    high = value.astype(bf16)
+    return high, (value - high.astype(f32)).astype(bf16)
+
+
+def spectrum_kernel(table_ref, kernel_ref, spec_ref):
+    table_high, table_low = halves(table_ref[...])
+    high, low = halves(kernel_ref[...])
+    spec_ref[...] = dot(table_high, high) + dot(table_low, high) + dot(table_high, low)
+
+
+def outer_kernel(meta_ref, sw0_ref, sw1_ref, sw2_ref, cot_ref, other_ref, acc_ref):
+    rows = sw0_ref.shape[0]
+    turned = (((0,), (0,)), ((), ()))
+    acc_ref[...] = (
+        lax.dot_general(sw0_ref[...], cot_ref[:rows], turned, preferred_element_type=f32)
+        + lax.dot_general(sw1_ref[...], cot_ref[rows:], turned, preferred_element_type=f32)
+        + lax.dot_general(sw2_ref[...], other_ref[...], turned, preferred_element_type=f32)
+    )
+
+
+def last_outer_kernel(meta_ref, acc_ref, sw_ref, cot_ref, own_ref, one_ref, two_ref, three_ref, total):
+    turned = (((0,), (0,)), ((), ()))
+    share = acc_ref.shape[0] // 4
+    piece = share // 4
+    for at in range(4):
+        rows = slice(at * share, (at + 1) * share)
+        total[rows] = acc_ref[rows] + lax.dot_general(
+            sw_ref[:, rows], cot_ref[...], turned, preferred_element_type=f32
+        )
+    core, place = meta_ref[1], meta_ref[2]
+    for shift, ref in enumerate((own_ref, one_ref, two_ref, three_ref)):
+        chunk = lax.rem(place + shift, 4)
+        for k in range(4):
+            start = jnp.where(core == 0, chunk * share + k * piece, k * share + chunk * piece)
+            value = total[pl.ds(pl.multiple_of(start, piece), piece)]
+            ref[k * piece : (k + 1) * piece] = value.astype(ref.dtype)
+
+
+def first_sum_kernel(meta_ref, a_ref, b_ref, c_ref, d_ref, own_ref, one_ref, two_ref, three_ref):
+    piece = own_ref.shape[0]
+    for shift, ref in enumerate((own_ref, one_ref, two_ref, three_ref)):
+        rows = pl.ds(pl.multiple_of(lax.rem(meta_ref[3] + shift, 4) * piece, piece), piece)
+        value = (a_ref[rows] + c_ref[rows].astype(f32)) + (b_ref[rows].astype(f32) + d_ref[rows].astype(f32))
+        ref[...] = value.astype(ref.dtype)
+
+
+def place_kernel(scale, meta_ref, *refs):
+    out_ref = refs[-1]
+    piece, width = refs[0].shape
+    for side in range(2):
+        core = meta_ref[1] if side == 0 else 1 - meta_ref[1]
+        place = meta_ref[4] if side == 0 else meta_ref[5]
+        cols = pl.ds(pl.multiple_of(core * width, width), width)
+        for shift in range(4):
+            rows = pl.ds(pl.multiple_of(lax.rem(place + 4 - shift, 4) * piece, piece), piece)
+            out_ref[rows, cols] = refs[side * 4 + shift][...] * scale
+
+
 def whole(shape):
-    return pl.BlockSpec(shape, lambda i: (0,) * len(shape))
+    return pl.BlockSpec(shape, lambda *i: (0,) * len(shape))
 
 
 SMEM = pl.BlockSpec(memory_space=pltpu.SMEM)
-
-
-def forward(meta, lengths, x, before, after, split, split_t, spec, gain, bias, interpret=False):
-    lanes, length, channels = x.shape
+VMEM = pl.BlockSpec(memory_space=pltpu.VMEM)
+
+
+def params(mebibytes):
+    return pltpu.CompilerParams(vmem_limit_bytes=mebibytes << 20)
+
+
+def cost(flops, moved):
+    return pl.CostEstimate(flops=flops, bytes_accessed=moved, transcendentals=0)
+
+
+def forward(lane, meta, lengths, flat, before, after, split, split_t, spec, gain, bias, interpret=False):
+    total, channels = flat.shape
+    lanes = lengths.shape[0]
+    length = total // lanes
     blocks = length // ROWS
-    steps = lanes * blocks
-    flat = x.reshape(lanes * length, channels)
     per = ROWS // EDGE
-    last = lanes * length // EDGE - 1
+    last = total // EDGE - 1
+    at = lane * blocks
     row = pl.BlockSpec((ROWS, channels), lambda i: (i, 0))
-    halo = pl.BlockSpec((EDGE, channels), lambda i: (i // blocks, 0))
+    halo = pl.BlockSpec((EDGE, channels), lambda i: (lane, 0))
     return pl.pallas_call(
-        functools.partial(forward_kernel, blocks),
-        grid=(steps,),
+        functools.partial(forward_kernel, lane, blocks),
+        grid=(blocks,),
         in_specs=[
             SMEM,
             SMEM,
-            row,
-            pl.BlockSpec((EDGE, channels), lambda i: (jnp.maximum(i * per - 1, 0), 0)),
-            pl.BlockSpec((EDGE, channels), lambda i: (jnp.minimum(i * per + per, last), 0)),
+            pl.BlockSpec((ROWS, channels), lambda i: (i + at, 0)),
+            pl.BlockSpec((EDGE, channels), lambda i: (jnp.maximum((i + at) * per - 1, 0), 0)),
+            pl.BlockSpec((EDGE, channels), lambda i: (jnp.minimum((i + at) * per + per, last), 0)),
             halo,
             halo,
             whole(split.shape),
@@ -239,44 +308,32 @@
             pl.BlockSpec((POINTS, channels), lambda i: (i, 0)),
         ],
         out_shape=[
-            jax.ShapeDtypeStruct((lanes * length, channels), bf16),
-            jax.ShapeDtypeStruct((lanes * length, channels), f32),
-            jax.ShapeDtypeStruct((lanes * length, 128), f32),
-            jax.ShapeDtypeStruct((steps * POINTS, channels), bf16),
+            jax.ShapeDtypeStruct((length, channels), bf16),
+            jax.ShapeDtypeStruct((length, channels), f32),
+            jax.ShapeDtypeStruct((length, 128), f32),
+            jax.ShapeDtypeStruct((blocks * POINTS, channels), bf16),
         ],
         scratch_shapes=[pltpu.VMEM((WINDOW, channels), bf16), pltpu.VMEM((ROWS, channels), f32)],
-        compiler_params=pltpu.CompilerParams(vmem_limit_bytes=40 << 20),
+        compiler_params=params(40),
+        cost_estimate=cost(length * channels * 2000, length * channels * 12),
         interpret=interpret,
-        name="conv_norm_swish",
-    )(
-        meta,
-        lengths,
-        flat,
-        flat,
-        flat,
-        before.reshape(lanes * EDGE, channels),
-        after.reshape(lanes * EDGE, channels),
-        split,
-        split_t,
-        spec,
-        gain,
-        bias,
-    )
-
-
-def backward(meta, lengths, cot, sw, normed, istd, xhat, w, split, split_t, spec, gather, gain, bias, lanes,
+        name=f"conv_norm_swish_{lane}",
+    )(meta, lengths, flat, flat, flat, before, after, split, split_t, spec, gain, bias)
+
+
+def backward(lane, meta, lengths, cot, sw, normed, istd, xhat, w, split, split_t, spec, gather, gain, bias,
              interpret=False):
-    total, channels = cot.shape
-    steps = total // ROWS
-    blocks = steps // lanes
+    total, channels = sw.shape
+    blocks = total // ROWS
+    at = lane * blocks
     row = pl.BlockSpec((ROWS, channels), lambda i: (i, 0))
     return pl.pallas_call(
-        functools.partial(backward_kernel, blocks),
-        grid=(steps,),
+        functools.partial(backward_kernel, lane, blocks),
+        grid=(blocks,),
         in_specs=[
             SMEM,
             SMEM,
-            row,
+            pl.BlockSpec((ROWS, channels), lambda i: (i + at, 0)),
             row,
             row,
             pl.BlockSpec((ROWS, 128), lambda i: (i, 0)),
@@ -289,11 +346,11 @@
             whole((1, channels)),
             whole((1, channels)),
         ],
-        out_specs=[row, whole((total, channels)), whole((lanes * 2 * EDGE, channels)), whole((40, channels))],
+        out_specs=[row, whole((total, channels)), whole((2 * EDGE, channels)), whole((40, channels))],
         out_shape=[
             jax.ShapeDtypeStruct((total, channels), bf16),
             jax.ShapeDtypeStruct((total, channels), bf16),
-            jax.ShapeDtypeStruct((lanes * 2 * EDGE, channels), bf16),
+            jax.ShapeDtypeStruct((2 * EDGE, channels), bf16),
             jax.ShapeDtypeStruct((40, channels), f32),
         ],
         scratch_shapes=[
@@ -304,59 +361,193 @@
             pltpu.VMEM((EDGE, channels), f32),
             pltpu.VMEM((EDGE, channels), f32),
         ],
-        compiler_params=pltpu.CompilerParams(vmem_limit_bytes=56 << 20),
+        compiler_params=params(56),
+        cost_estimate=cost(total * channels * 8000, total * channels * 20),
         interpret=interpret,
-        name="backward",
+        name=f"backward_{lane}",
     )(meta, lengths, cot, sw, normed, istd, xhat, w, split, split_t, spec, gather, gain, bias)
+
+
+def outer(meta, sw0, sw1, sw2, cot, other):
+    rows, channels = sw0.shape
+    width = channels // 2
+    share = channels // 4
+    left = pl.BlockSpec((rows, share), lambda i, meta: (0, i))
+    return pl.pallas_call(
+        outer_kernel,
+        grid_spec=pltpu.PrefetchScalarGridSpec(
+            num_scalar_prefetch=1,
+            grid=(4,),
+            in_specs=[
+                left,
+                left,
+                left,
+                pl.BlockSpec((2 * rows, width), lambda i, meta: (0, meta[1])),
+                pl.BlockSpec((rows, width), lambda i, meta: (0, meta[1])),
+            ],
+            out_specs=pl.BlockSpec((share, width), lambda i, meta: (i, 0)),
+        ),
+        out_shape=jax.ShapeDtypeStruct((channels, width), f32),
+        compiler_params=params(40),
+        cost_estimate=cost(6 * rows * channels * width, 10 * rows * channels),
+        name="outer_most",
+    )(meta, sw0, sw1, sw2, cot, other)
+
+
+def last_outer(meta, acc, sw, cot):
+    rows, channels = sw.shape
+    width, share = channels // 2, channels // 4
+    return pl.pallas_call(
+        last_outer_kernel,
+        grid_spec=pltpu.PrefetchScalarGridSpec(
+            num_scalar_prefetch=1,
+            grid=(1,),
+            in_specs=[
+                whole(acc.shape),
+                whole(sw.shape),
+                pl.BlockSpec((rows, width), lambda i, meta: (1, meta[1])),
+            ],
+            out_specs=[whole((share, width))] * 4,
+            scratch_shapes=[pltpu.VMEM(acc.shape, f32)],
+        ),
+        out_shape=[jax.ShapeDtypeStruct((share, width), d) for d in (f32, bf16, bf16, bf16)],
+        compiler_params=params(40),
+        cost_estimate=cost(2 * rows * channels * width, 10 * rows * channels),
+        name="outer_last",
+    )(meta, acc, sw, cot)
+
+
+def first_sum(meta, parts):
+    share, width = parts[0].shape
+    piece = share // 4
+    return pl.pallas_call(
+        first_sum_kernel,
+        in_specs=[SMEM] + [VMEM] * 4,
+        out_specs=[VMEM] * 4,
+        out_shape=[jax.ShapeDtypeStruct((piece, width), d) for d in (f32, bf16, bf16, bf16)],
+        compiler_params=params(32),
+        name="sum_first",
+    )(meta, *parts)
+
+
+def place(meta, pieces, scale):
+    piece, width = pieces[0].shape
+    return pl.pallas_call(
+        functools.partial(place_kernel, scale),
+        in_specs=[SMEM] + [VMEM] * 8,
+        out_specs=VMEM,
+        out_shape=jax.ShapeDtypeStruct((4 * piece, 2 * width), f32),
+        compiler_params=params(32),
+        name="place",
+    )(meta, *pieces)
 
 
 def shifts(size):
     up = [(i, i + 1) for i in range(size - 1)]
     return up, [(j, i) for i, j in up]
+
+
+EVERY = ("dp", "seq")
+
+
+def along(axes, shift):
+    pairs = []
+    for device in range(128):
+        where = {"y": device % 4, "c": device // 4 % 2, "x": device // 8 % 4, "z": device // 32}
+        axis = axes[where["c"]]
+        moved = dict(where)
+        moved[axis] = (where[axis] + shift) % (2 if axis == "c" else 4)
+        pairs.append((device, ((moved["z"] * 4 + moved["x"]) * 2 + moved["c"]) * 4 + moved["y"]))
+    return pairs
+
+
+def swap(value):
+    return lax.ppermute(value, EVERY, along("cc", 1))
+
+
+def spread(values, axes):
+    return [lax.ppermute(value, EVERY, along(axes, s + 1)) for s, value in enumerate(values)]
+
+
+def four(own, one, two, three):
+    own, one, two, three = (v.astype(f32) for v in (own, one, two, three))
+    return (own + two) + (one + three)
+
+
+def all_four(value, axes):
+    return four(value, *spread([value] * 3, axes))
 
 
 def local(glu_out, lengths, kernel, norm_gain, norm_bias, w_out, cotangent, interpret=False):
     lanes, length, channels = glu_out.shape
     seq_count = lax.axis_size("seq")
     norm_scale = 1.0 / math.sqrt(lanes * lax.axis_size("dp") * length * seq_count)
-    seq_place = lax.axis_index("seq")
+    y = lax.axis_index("seq")
+    dp = lax.axis_index("dp")
+    core, x, z = lax.rem(dp, 2), lax.rem(lax.div(dp, 2), 4), lax.div(dp, 8)
+    first = core == 0
+    meta = jnp.stack(
+        [
+            y * length,
+            core,
+            jnp.where(first, y, z),
+            jnp.where(first, x, y),
+            jnp.where(first, x, z),
+            jnp.where(first, z, x),
+        ]
+    ).astype(jnp.int32)
     up, down = shifts(seq_count)
-    before = lax.ppermute(glu_out[:, length - EDGE :], "seq", up)
-    after = lax.ppermute(glu_out[:, :EDGE], "seq", down)
-    split, spectrum, gather = tables()
-    spec = jnp.dot(jnp.asarray(spectrum), kernel, precision=lax.Precision.HIGHEST)
-    split_t = jnp.asarray(np.ascontiguousarray(split.T))
-    split = jnp.asarray(split)
-    table = np.zeros((32, 3 * BINS), np.float32)
-    table[:TAPS] = gather.T
+    before = lax.ppermute(glu_out[:, length - EDGE :], "seq", up).reshape(lanes * EDGE, channels)
+    after = lax.ppermute(glu_out[:, :EDGE], "seq", down).reshape(lanes * EDGE, channels)
+    cot = cotangent.reshape(-1, channels)
+    cot_other = swap(cot)
+    split, split_t, wide, deep = (jnp.asarray(t) for t in tables())
+    spec = pl.pallas_call(
+        spectrum_kernel,
+        out_shape=jax.ShapeDtypeStruct((3 * BINS, channels), f32),
+        compiler_params=params(32),
+        interpret=interpret,
+        name="spectrum",
+    )(wide, jnp.pad(kernel, ((0, 32 - TAPS), (0, 0))))
     gain, bias = norm_gain.reshape(1, channels), norm_bias.reshape(1, channels)
-    meta = jnp.reshape(seq_place * length, (1,)).astype(jnp.int32)
-    sw, normed, istd, xhat = forward(
-        meta, lengths, glu_out, before, after, split, split_t, spec, gain, bias, interpret=interpret
-    )
-    cot = cotangent.reshape(-1, channels)
-    outer = lax.dot_general(sw, cot, (((0,), (0,)), ((), ())), preferred_element_type=f32)
-    summed = lax.psum(outer, ("dp", "seq"))
-    share = channels // seq_count
-    grad_w = lax.dynamic_slice_in_dim(summed, seq_place * share, share, 0) * norm_scale
-    layer, gi, edge, small = backward(
-        meta, lengths, cot, sw, normed, istd, xhat, w_out, split, split_t, spec, jnp.asarray(table), gain, bias, lanes,
-        interpret=interpret,
-    )
-    edge = edge.reshape(lanes, 2, EDGE, channels)
-    from_after = lax.ppermute(edge[:, 0], "seq", down)
-    from_before = lax.ppermute(edge[:, 1], "seq", up)
-    gi = gi.reshape(lanes, length, channels)
+    flat = glu_out.reshape(lanes * length, channels)
+    ahead = [
+        forward(lane, meta, lengths, flat, before, after, split, split_t, spec, gain, bias, interpret=interpret)
+        for lane in range(lanes)
+    ]
+    swished = [a[0] for a in ahead]
+    other = [swap(s) for s in swished]
+    acc = outer(meta, swished[0], swished[1], other[0], cot, cot_other)
+    parts = last_outer(meta, acc, other[1], cot_other)
+    parts = [parts[0]] + spread(parts[1:], "yz")
+    back = [
+        backward(lane, meta, lengths, cot, *ahead[lane], w_out, split, split_t, spec, deep, gain, bias,
+                 interpret=interpret)
+        for lane in range(lanes)
+    ]
+    pieces = first_sum(meta, parts)
+    pieces = [pieces[0]] + spread(pieces[1:], "xy")
+    piece = all_four(four(*pieces).astype(bf16), "zx")
+    pieces = [piece] + spread([piece] * 3, "xz")
+    grad_w = place(meta, pieces + [swap(p) for p in pieces], norm_scale)
+
+    layer = jnp.stack([b[0] for b in back])
+    gi = jnp.stack([b[1] for b in back])
+    edge = jnp.stack([b[2] for b in back])
+    from_after = lax.ppermute(edge[:, :EDGE], "seq", down)
+    from_before = lax.ppermute(edge[:, EDGE:], "seq", up)
     gi = gi.at[:, :EDGE].add(from_before).at[:, length - EDGE :].add(from_after)
-    small = lax.psum(small, ("dp", "seq")) * norm_scale
-    return (
-        layer.reshape(lanes, length, channels),
-        gi,
-        grad_w,
-        small[:TAPS],
-        small[32],
-        small[33],
-    )
+
+    small = back[0][3] + back[1][3]
+    small = small + swap(small)
+    half = channels // 2
+    small = lax.dynamic_slice_in_dim(small, core * half, half, 1)
+    for axes in ("yz", "xy", "zx"):
+        small = all_four(small, axes)
+    small = small * norm_scale
+    away = swap(small)
+    small = jnp.concatenate([jnp.where(first, small, away), jnp.where(first, away, small)], axis=1)
+    return (layer, gi, grad_w, small[:TAPS], small[32], small[33])
 
 
 def solution(mesh):

time: 272 us -> 189 us (0.69)
  waiting for transfers between devices: 159 us -> 7.54 us
  starting transfers between devices: 10.6 us -> 69.3 us
  Pallas kernels: 59.4 us -> 81.9 us
  between operations: 14.2 us -> 1 us
  matrix products: 12 us -> 0 us
  local copies, waits for them, and re-layouts: 9 us -> 21 us
    psum x1 -> x0, waiting for transfers between devices: 156 us -> none  [local(): summed = lax.psum(outer, ('dp', 'seq'))]
    ppermute x4 -> x34, starting transfers between devices: 10.6 us -> 69.3 us  [the longest x21 34.9 us: spread(): lax.ppermute(value, EVERY, along(axes, s + 1))]
    pallas_call x2 -> x9, Pallas kernels: 59.4 us -> 81.9 us  [the longest x2 48.5 us: backward(): pl.pallas_call(functools.partial(backward_kernel, lane, blocks), grid=(bl...]
    dot_general x2 -> x0, matrix products: 12 us -> none  [the longest x1 7.71 us: local(): lax.dot_general(sw, cot, (((0,), (0,)), ((), ())), preferred_element_type...]
    unnamed x26 -> x56, local copies, waits for them, and re-layouts: 5.18 us -> 16.9 us
    ppermute x4 -> x34, waiting for transfers between devices: 2.51 us -> 7.54 us  [the longest x21 7.5 us: spread(): lax.ppermute(value, EVERY, along(axes, s + 1))]
    another operation x0 -> x3, other arithmetic: none -> 4.62 us  [the longest x1 1.94 us: local(): layer = jnp.stack([b[0] for b in back])]
    mul x2 -> x1, other arithmetic: 4.25 us -> 0.04 us  [local(): small = small * norm_scale]
  transfers between devices with their start and end apart: 5 -> 34, of which waited for: 3 -> 4; matrix products, arithmetic and copies ran while one was open for 3% -> 6% of each run, Pallas kernels for 0% -> 42%
where the time goes in v2:
time: 189 us; the launch traced here: 188 us
  Pallas kernels  81.9 us (43%)
  starting transfers between devices  69.3 us (37%)
  local copies, waits for them, and re-layouts  21 us (11%)
  waiting for transfers between devices  7.54 us (4%)
  other arithmetic  7.29 us (4%)
    pallas_call x2, Pallas kernels, backward(): pl.pallas_call(functools.partial(backward_kernel, lane, blocks), grid=(bl...  48.5 us
    ppermute x21, starting transfers between devices, spread(): lax.ppermute(value, EVERY, along(axes, s + 1))  34.9 us
    ppermute x9, starting transfers between devices, swap(): return lax.ppermute(value, EVERY, along('cc', 1))  24.2 us
    pallas_call x2, Pallas kernels, forward(): pl.pallas_call(functools.partial(forward_kernel, lane, blocks), grid=(blo...  17.8 us
    unnamed x56, local copies, waits for them, and re-layouts  16.9 us
    pallas_call x1, Pallas kernels, outer(): pl.pallas_call(outer_kernel, grid_spec=pltpu.PrefetchScalarGridSpec(num_s...  7.89 us
    ppermute x21, waiting for transfers between devices, spread(): lax.ppermute(value, EVERY, along(axes, s + 1))  7.5 us
    ppermute x1, starting transfers between devices, local(): from_before = lax.ppermute(edge[:, EDGE:], 'seq', up)  4.22 us
  transfers between devices with their start and end apart: 34, of which 4 were waited for; matrix products, arithmetic and copies ran while one was open for 6% of the time, Pallas kernels for 42%

profile of v2, /device:TPU:1, one launch (start us, length us, event | category | flops | bytes accessed | tf_op | source)
XLA Modules:
  0.0 188.0 jit_solution(15749625319812990381)
XLA Ops:
  3.8 3.5 %collective-permute-start = (bf16[2,16,1536]{2,1,0:T(8,128)(2,1)}, bf16[2,16,1536]{2,1,0:T(8,128)(2,1)S(1)}, u32[]{:S(2)}, u32[]{:S(2)}) collective-permute-start(bf16[2,16,1536]{2,1,0:T(8,128)(2,1)} %get-tuple-element.81), channel_id=1, source_target_pairs={{0,1},{1,2},{2,3},{4,5},{5,6},{6,7},{8,9},{9,10},{10,11},{12,13},{... | collective-permute-start | bytes 294920 | tf_op jit(solution)/shard_map/ppermute | solution.py:500
  14.5 1.7 copy-done.2
  17.8 8.4 %conv_norm_swish_0.1 = (bf16[512,1536]{1,0:T(8,128)(2,1)S(1)}, f32[512,1536]{1,0:T(8,128)S(1)}, f32[512,128]{1,0:T(8,128)S(1)}, bf16[1024,1536]{1,0:T(8,128)(2,1)S(1)}) custom-call(s32[6]{0:T(128)S(1)} %stack.54.meta_ref, s32[2,8]{1,0:T(2,128)S(1)} %copy-done.14, bf16[1024,1536]{1,0:T(8,128)(2,1)S(1)} %bitcast.16, bf16[1024,1536]{1,0:T(8,128)(2,1)S(1)} %bitcast.17, ...), custom_call_target="tpu_custom_call" | custom-call | flops 1572864000 | bytes 9437184 | tf_op jit(solution)/shard_map/conv_norm_swish_0/pallas_call | solution.py:287
  27.9 1.6 copy-done.18
  30.5 9.3 %conv_norm_swish_1.1 = (bf16[512,1536]{1,0:T(8,128)(2,1)}, f32[512,1536]{1,0:T(8,128)S(1)}, f32[512,128]{1,0:T(8,128)S(1)}, bf16[1024,1536]{1,0:T(8,128)(2,1)S(1)}) custom-call(s32[6]{0:T(128)S(1)} %stack.54.meta_ref, s32[2,8]{1,0:T(2,128)S(1)} %copy-done.14, bf16[1024,1536]{1,0:T(8,128)(2,1)S(1)} %bitcast.19, bf16[1024,1536]{1,0:T(8,128)(2,1)S(1)} %bitcast.20, ...), custom_call_target="tpu_custom_call" | custom-call | flops 1572864000 | bytes 9437184 | tf_op jit(solution)/shard_map/conv_norm_swish_1/pallas_call | solution.py:287
  39.8 1.7 copy-done.15
  41.5 1.7 copy-done.16
  44.1 24.2 %backward_0.1 = (bf16[512,1536]{1,0:T(8,128)(2,1)}, bf16[512,1536]{1,0:T(8,128)(2,1)}, bf16[32,1536]{1,0:T(8,128)(2,1)}, f32[40,1536]{1,0:T(8,128)}) custom-call(s32[6]{0:T(128)} %copy-done.12, s32[2,8]{1,0:T(2,128)} %lengths_ref.7, bf16[1024,1536]{1,0:T(8,128)(2,1)} %bitcast.23, bf16[512,1536]{1,0:T(8,128)(2,1)} %copy-done.5, f32[512,1536]{1,0:T(8,128)} %copy-done.17, ...), custom_call_target="tpu_custom_call" | custom-call | flops 6291456000 | bytes 15728640 | tf_op jit(solution)/shard_map/backward_0/pallas_call | solution.py:330
  68.4 24.2 %backward_1.1 = (bf16[512,1536]{1,0:T(8,128)(2,1)}, bf16[512,1536]{1,0:T(8,128)(2,1)}, bf16[32,1536]{1,0:T(8,128)(2,1)}, f32[40,1536]{1,0:T(8,128)}) custom-call(s32[6]{0:T(128)} %copy-done.12, s32[2,8]{1,0:T(2,128)} %lengths_ref.7, bf16[1024,1536]{1,0:T(8,128)(2,1)} %bitcast.24, bf16[512,1536]{1,0:T(8,128)(2,1)} %get-tuple-element.59.sw_ref.sw1_ref, ...), custom_call_target="tpu_custom_call" | custom-call | flops 6291456000 | bytes 15728640 | tf_op jit(solution)/shard_map/backward_1/pallas_call | solution.py:330
  94.7 4.2 %collective-permute-start.2 = (bf16[2,16,1536]{2,1,0:T(8,128)(2,1)S(1)}, bf16[2,16,1536]{2,1,0:T(8,128)(2,1)S(1)}, u32[]{:S(2)}, u32[]{:S(2)}) collective-permute-start(bf16[2,16,1536]{2,1,0:T(8,128)(2,1)S(1)} %get-tuple-element.85), channel_id=1, source_target_pairs={{0,1},{1,2},{2,3},{4,5},{5,6},{6,7},{8,9},{9,10},{10,11},{12,13},{... | collective-permute-start | bytes 294920 | tf_op jit(solution)/shard_map/ppermute | solution.py:538
  99.0 1.8 pad_maximum_fusion
  101.8 7.9 %outer_most.1.acc_ref = f32[1536,768]{1,0:T(8,128)} custom-call(s32[6]{0:T(128)S(1)} %copy-done.13, bf16[512,1536]{1,0:T(8,128)(2,1)S(1)} %copy-done.6, bf16[512,1536]{1,0:T(8,128)(2,1)} %get-tuple-element.59.sw_ref.sw1_ref, bf16[512,1536]{1,0:T(8,128)(2,1)S(1)} %collective-permute-done.4.sw2_ref, bf16[1024,1536]{1,0:T(8,128)(2,1)S(1)} %bitcast.25, ...), custom_call_target="tpu_custom_call" | custom-call | flops 3623878656 | bytes 7864320 | tf_op jit(solution)/shard_map/outer_most/pallas_call | solution.py:376
  109.7 2.3 %copy-done.3 = f32[1536,768]{1,0:T(8,128)S(1)} copy-done((f32[1536,768]{1,0:T(8,128)S(1)}, f32[1536,768]{1,0:T(8,128)}, u32[]{:S(2)}) %copy-start.3) | copy-done | bytes 4718616
  112.0 3.7 %outer_last.1 = (f32[384,768]{1,0:T(8,128)S(1)}, bf16[384,768]{1,0:T(8,128)(2,1)S(1)}, bf16[384,768]{1,0:T(8,128)(2,1)S(1)}, bf16[384,768]{1,0:T(8,128)(2,1)S(1)}) custom-call(s32[6]{0:T(128)S(1)} %copy-done.13, f32[1536,768]{1,0:T(8,128)S(1)} %copy-done.3, bf16[512,1536]{1,0:T(8,128)(2,1)S(1)} %collective-permute-done.6.sw_ref, ...), custom_call_target="tpu_custom_call" | custom-call | flops 1207959552 | bytes 7864320 | tf_op jit(solution)/shard_map/outer_last/pallas_call | solution.py:400
  115.7 1.7 collective-permute-start.7
  117.4 3.4 %collective-permute-start.24 = (f32[40,768]{1,0:T(8,128)S(1)}, f32[40,768]{1,0:T(8,128)S(1)}, u32[]{:S(2)}, u32[]{:S(2)}) collective-permute-start(f32[40,768]{1,0:T(8,128)S(1)} %dynamic-slice_add_fusion), channel_id=1, source_target_pairs={{0,2},{1,3},{2,0},{3,1},{4,68},{5,69},{6,70},{7,71},{8,10},{9,11},... | collective-permute-start | bytes 368648 | tf_op jit(solution)/shard_map/ppermute | solution.py:469
  120.8 2.7 %collective-permute-start.26 = (f32[40,768]{1,0:T(8,128)S(1)}, f32[40,768]{1,0:T(8,128)S(1)}, u32[]{:S(2)}, u32[]{:S(2)}) collective-permute-start(f32[40,768]{1,0:T(8,128)S(1)} %dynamic-slice_add_fusion), channel_id=1, source_target_pairs={{0,3},{1,0},{2,1},{3,2},{4,100},{5,101},{6,102},{7,103},{8,11},{9,... | collective-permute-start | bytes 368648 | tf_op jit(solution)/shard_map/ppermute | solution.py:469
  123.5 1.9 %pad_maximum_fusion.1 = bf16[2,512,1536]{2,1,0:T(8,128)(2,1)} fusion(bf16[1,512,1536]{2,1,0:T(8,128)(2,1)S(1)} %bitcast.33, bf16[1,512,1536]{2,1,0:T(8,128)(2,1)S(1)} %bitcast.32), kind=kLoop, calls=%fused_computation.3 | loop fusion | flops 1572864 | bytes 6291456 | tf_op jit(solution)/shard_map/stack | solution.py:534
  125.5 4.0 %collective-permute-done.24 = f32[40,768]{1,0:T(8,128)S(1)} collective-permute-done((f32[40,768]{1,0:T(8,128)S(1)}, f32[40,768]{1,0:T(8,128)S(1)}, u32[]{:S(2)}, u32[]{:S(2)}) %collective-permute-start.24) | collective-permute-done | bytes 122912 | tf_op jit(solution)/shard_map/ppermute | solution.py:469
  129.5 1.8 collective-permute-start.9
  131.3 3.3 %collective-permute-start.27 = (f32[40,768]{1,0:T(8,128)S(1)}, f32[40,768]{1,0:T(8,128)S(1)}, u32[]{:S(2)}, u32[]{:S(2)}) collective-permute-start(f32[40,768]{1,0:T(8,128)S(1)} %add_add_fusion.2), channel_id=1, source_target_pairs={{0,16},{1,17},{2,18},{3,19},{4,6},{5,7},{6,4},{7,5},{8,24},{9,25},... | collective-permute-start | bytes 368648 | tf_op jit(solution)/shard_map/ppermute | solution.py:469
  134.6 2.7 %collective-permute-start.29 = (f32[40,768]{1,0:T(8,128)S(1)}, f32[40,768]{1,0:T(8,128)S(1)}, u32[]{:S(2)}, u32[]{:S(2)}) collective-permute-start(f32[40,768]{1,0:T(8,128)S(1)} %add_add_fusion.2), channel_id=1, source_target_pairs={{0,24},{1,25},{2,26},{3,27},{4,7},{5,4},{6,5},{7,6},{8,0},{9,1},{1... | collective-permute-start | bytes 368648 | tf_op jit(solution)/shard_map/ppermute | solution.py:469
  137.3 2.6 %collective-permute-done.8.c_ref = bf16[384,768]{1,0:T(8,128)(2,1)S(1)} collective-permute-done((bf16[384,768]{1,0:T(8,128)(2,1)S(1)}, bf16[384,768]{1,0:T(8,128)(2,1)S(1)}, u32[]{:S(2)}, u32[]{:S(2)}) %collective-permute-start.8) | collective-permute-done | bytes 589856 | tf_op jit(solution)/shard_map/ppermute | solution.py:469
  142.1 3.6 %collective-permute-start.10 = (bf16[96,768]{1,0:T(8,128)(2,1)S(1)}, bf16[96,768]{1,0:T(8,128)(2,1)S(1)}, u32[]{:S(2)}, u32[]{:S(2)}) collective-permute-start(bf16[96,768]{1,0:T(8,128)(2,1)S(1)} %get-tuple-element.73), channel_id=1, source_target_pairs={{0,16},{1,17},{2,18},{3,19},{4,6},{5,7},{6,4},{7,5},{8,24},{9,25},... | collective-permute-start | bytes 442376 | tf_op jit(solution)/shard_map/ppermute | solution.py:469
  146.6 1.8 collective-permute-start.12
  148.5 2.8 %collective-permute-start.30 = (f32[40,768]{1,0:T(8,128)S(1)}, f32[40,768]{1,0:T(8,128)S(1)}, u32[]{:S(2)}, u32[]{:S(2)}) collective-permute-start(f32[40,768]{1,0:T(8,128)S(1)} %add_add_fusion.1), channel_id=1, source_target_pairs={{0,64},{1,65},{2,66},{3,67},{4,20},{5,21},{6,22},{7,23},{8,72},{9,... | collective-permute-start | bytes 368648 | tf_op jit(solution)/shard_map/ppermute | solution.py:469
  151.6 2.4 %collective-permute-start.32 = (f32[40,768]{1,0:T(8,128)S(1)}, f32[40,768]{1,0:T(8,128)S(1)}, u32[]{:S(2)}, u32[]{:S(2)}) collective-permute-start(f32[40,768]{1,0:T(8,128)S(1)} %add_add_fusion.1), channel_id=1, source_target_pairs={{0,96},{1,97},{2,98},{3,99},{4,28},{5,29},{6,30},{7,31},{8,104},{9... | collective-permute-start | bytes 368648 | tf_op jit(solution)/shard_map/ppermute | solution.py:469
  157.8 10.5 %collective-permute-start.33 = (f32[40,768]{1,0:T(8,128)S(1)}, f32[40,768]{1,0:T(8,128)S(1)}, u32[]{:S(2)}, u32[]{:S(2)}) collective-permute-start(f32[40,768]{1,0:T(8,128)S(1)} %add_multiply_fusion), channel_id=1, source_target_pairs={{0,4},{1,5},{2,6},{3,7},{4,0},{5,1},{6,2},{7,3},{8,12},{9,13},{10,... | collective-permute-start | bytes 368648 | tf_op jit(solution)/shard_map/ppermute | solution.py:465
  168.5 4.5 %collective-permute-start.17 = (f32[96,768]{1,0:T(8,128)S(1)}, f32[96,768]{1,0:T(8,128)S(1)}, u32[]{:S(2)}, u32[]{:S(2)}) collective-permute-start(f32[96,768]{1,0:T(8,128)S(1)} %add_add_fusion.refs_0_), channel_id=1, source_target_pairs={{0,16},{1,17},{2,18},{3,19},{4,68},{5,69},{6,70},{7,71},{8,24},{9,... | collective-permute-start | bytes 884744 | tf_op jit(solution)/shard_map/ppermute | solution.py:469
  173.1 2.9 %collective-permute-start.19 = (f32[96,768]{1,0:T(8,128)S(1)}, f32[96,768]{1,0:T(8,128)S(1)}, u32[]{:S(2)}, u32[]{:S(2)}) collective-permute-start(f32[96,768]{1,0:T(8,128)S(1)} %add_add_fusion.refs_0_), channel_id=1, source_target_pairs={{0,4},{1,5},{2,6},{3,7},{4,0},{5,1},{6,2},{7,3},{8,12},{9,13},{10,... | collective-permute-start | bytes 884744 | tf_op jit(solution)/shard_map/ppermute | solution.py:465
  176.0 7.6 %collective-permute-start.20 = (f32[96,768]{1,0:T(8,128)S(1)}, f32[96,768]{1,0:T(8,128)S(1)}, u32[]{:S(2)}, u32[]{:S(2)}) collective-permute-start(f32[96,768]{1,0:T(8,128)S(1)} %collective-permute-done.16.refs_1_), channel_id=1, source_target_pairs={{0,4},{1,5},{2,6},{3,7},{4,0},{5,1},{6,2},{7,3},{8,12},{9,13},{10,... | collective-permute-start | bytes 884744 | tf_op jit(solution)/shard_map/ppermute | solution.py:465
  185.9 2.2 %place.1 = f32[384,1536]{1,0:T(8,128)} custom-call(s32[6]{0:T(128)S(1)} %copy-done.13, f32[96,768]{1,0:T(8,128)S(1)} %add_add_fusion.refs_0_, f32[96,768]{1,0:T(8,128)S(1)} %collective-permute-done.16.refs_1_, f32[96,768]{1,0:T(8,128)S(1)} %collective-permute-done.17.refs_2_, f32[96,768]{1,0:T(8,128)S(1)} %collective-permute-done.18.refs_3_, ...), custom_call_target="tpu_custom_call" | custom-call | tf_op jit(solution)/shard_map/place/pallas_call | solution.py:435
  (121 shorter events, 28.3 us)
Async XLA Ops:
  0.7 100.2 %collective-permute-start.5 = (bf16[1024,1536]{1,0:T(8,128)(2,1)}, bf16[1024,1536]{1,0:T(8,128)(2,1)}, u32[]{:S(2)}, u32[]{:S(2)}) collective-permute-start(bf16[1024,1536]{1,0:T(8,128)(2,1)} %bitcast.22), channel_id=1, source_target_pairs={{0,4},{1,5},{2,6},{3,7},{4,0},{5,1},{6,2},{7,3},{8,12},{9,13},{10,... | collective-permute-start | bytes 9437192 | tf_op jit(solution)/shard_map/ppermute | solution.py:465
  3.8 10.7 %collective-permute-start = (bf16[2,16,1536]{2,1,0:T(8,128)(2,1)}, bf16[2,16,1536]{2,1,0:T(8,128)(2,1)S(1)}, u32[]{:S(2)}, u32[]{:S(2)}) collective-permute-start(bf16[2,16,1536]{2,1,0:T(8,128)(2,1)} %get-tuple-element.81), channel_id=1, source_target_pairs={{0,1},{1,2},{2,3},{4,5},{5,6},{6,7},{8,9},{9,10},{10,11},{12,13},{... | collective-permute-start | bytes 294920 | tf_op jit(solution)/shard_map/ppermute | solution.py:500
  7.3 7.2 %collective-permute-start.1 = (bf16[2,16,1536]{2,1,0:T(8,128)(2,1)}, bf16[2,16,1536]{2,1,0:T(8,128)(2,1)}, u32[]{:S(2)}, u32[]{:S(2)}) collective-permute-start(bf16[2,16,1536]{2,1,0:T(8,128)(2,1)} %get-tuple-element.80), channel_id=1, source_target_pairs={{1,0},{2,1},{3,2},{5,4},{6,5},{7,6},{9,8},{10,9},{11,10},{13,12},{... | collective-permute-start | bytes 294920 | tf_op jit(solution)/shard_map/ppermute | solution.py:501
  30.2 70.6 %collective-permute-start.4 = (bf16[512,1536]{1,0:T(8,128)(2,1)S(1)}, bf16[512,1536]{1,0:T(8,128)(2,1)S(1)}, u32[]{:S(2)}, u32[]{:S(2)}) collective-permute-start(bf16[512,1536]{1,0:T(8,128)(2,1)S(1)} %get-tuple-element.54.sw_ref.sw0_ref), channel_id=1, source_target_pairs={{0,4},{1,5},{2,6},{3,7},{4,0},{5,1},{6,2},{7,3},{8,12},{9,13},{10,... | collective-permute-start | bytes 4718600 | tf_op jit(solution)/shard_map/ppermute | solution.py:465
  43.8 65.9 %collective-permute-start.6 = (bf16[512,1536]{1,0:T(8,128)(2,1)}, bf16[512,1536]{1,0:T(8,128)(2,1)S(1)}, u32[]{:S(2)}, u32[]{:S(2)}) collective-permute-start(bf16[512,1536]{1,0:T(8,128)(2,1)} %get-tuple-element.59.sw_ref.sw1_ref), channel_id=1, source_target_pairs={{0,4},{1,5},{2,6},{3,7},{4,0},{5,1},{6,2},{7,3},{8,12},{9,13},{10,... | collective-permute-start | bytes 4718600 | tf_op jit(solution)/shard_map/ppermute | solution.py:465
  93.6 23.8 %collective-permute-start.23 = (f32[40,1536]{1,0:T(8,128)S(1)}, f32[40,1536]{1,0:T(8,128)S(1)}, u32[]{:S(2)}, u32[]{:S(2)}) collective-permute-start(f32[40,1536]{1,0:T(8,128)S(1)} %add.78), channel_id=1, source_target_pairs={{0,4},{1,5},{2,6},{3,7},{4,0},{5,1},{6,2},{7,3},{8,12},{9,13},{10,... | collective-permute-start | bytes 737288 | tf_op jit(solution)/shard_map/ppermute | solution.py:465
  94.7 39.9 %collective-permute-start.2 = (bf16[2,16,1536]{2,1,0:T(8,128)(2,1)S(1)}, bf16[2,16,1536]{2,1,0:T(8,128)(2,1)S(1)}, u32[]{:S(2)}, u32[]{:S(2)}) collective-permute-start(bf16[2,16,1536]{2,1,0:T(8,128)(2,1)S(1)} %get-tuple-element.85), channel_id=1, source_target_pairs={{0,1},{1,2},{2,3},{4,5},{5,6},{6,7},{8,9},{9,10},{10,11},{12,13},{... | collective-permute-start | bytes 294920 | tf_op jit(solution)/shard_map/ppermute | solution.py:538
  115.7 18.9 %collective-permute-start.7 = (bf16[384,768]{1,0:T(8,128)(2,1)S(1)}, bf16[384,768]{1,0:T(8,128)(2,1)S(1)}, u32[]{:S(2)}, u32[]{:S(2)}) collective-permute-start(bf16[384,768]{1,0:T(8,128)(2,1)S(1)} %get-tuple-element.69), channel_id=1, source_target_pairs={{0,1},{1,2},{2,3},{3,0},{4,36},{5,37},{6,38},{7,39},{8,9},{9,10},{... | collective-permute-start | bytes 1769480 | tf_op jit(solution)/shard_map/ppermute | solution.py:469
  117.4 12.0 %collective-permute-start.24 = (f32[40,768]{1,0:T(8,128)S(1)}, f32[40,768]{1,0:T(8,128)S(1)}, u32[]{:S(2)}, u32[]{:S(2)}) collective-permute-start(f32[40,768]{1,0:T(8,128)S(1)} %dynamic-slice_add_fusion), channel_id=1, source_target_pairs={{0,2},{1,3},{2,0},{3,1},{4,68},{5,69},{6,70},{7,71},{8,10},{9,11},... | collective-permute-start | bytes 368648 | tf_op jit(solution)/shard_map/ppermute | solution.py:469
  120.8 8.6 %collective-permute-start.25 = (f32[40,768]{1,0:T(8,128)S(1)}, f32[40,768]{1,0:T(8,128)S(1)}, u32[]{:S(2)}, u32[]{:S(2)}) collective-permute-start(f32[40,768]{1,0:T(8,128)S(1)} %dynamic-slice_add_fusion), channel_id=1, source_target_pairs={{0,1},{1,2},{2,3},{3,0},{4,36},{5,37},{6,38},{7,39},{8,9},{9,10},{... | collective-permute-start | bytes 368648 | tf_op jit(solution)/shard_map/ppermute | solution.py:469
  120.8 10.4 %collective-permute-start.26 = (f32[40,768]{1,0:T(8,128)S(1)}, f32[40,768]{1,0:T(8,128)S(1)}, u32[]{:S(2)}, u32[]{:S(2)}) collective-permute-start(f32[40,768]{1,0:T(8,128)S(1)} %dynamic-slice_add_fusion), channel_id=1, source_target_pairs={{0,3},{1,0},{2,1},{3,2},{4,100},{5,101},{6,102},{7,103},{8,11},{9,... | collective-permute-start | bytes 368648 | tf_op jit(solution)/shard_map/ppermute | solution.py:469
  129.4 10.5 %collective-permute-start.8 = (bf16[384,768]{1,0:T(8,128)(2,1)S(1)}, bf16[384,768]{1,0:T(8,128)(2,1)S(1)}, u32[]{:S(2)}, u32[]{:S(2)}) collective-permute-start(bf16[384,768]{1,0:T(8,128)(2,1)S(1)} %get-tuple-element.70), channel_id=1, source_target_pairs={{0,2},{1,3},{2,0},{3,1},{4,68},{5,69},{6,70},{7,71},{8,10},{9,11},... | collective-permute-start | bytes 1769480 | tf_op jit(solution)/shard_map/ppermute | solution.py:469
  129.5 11.8 %collective-permute-start.9 = (bf16[384,768]{1,0:T(8,128)(2,1)S(1)}, bf16[384,768]{1,0:T(8,128)(2,1)S(1)}, u32[]{:S(2)}, u32[]{:S(2)}) collective-permute-start(bf16[384,768]{1,0:T(8,128)(2,1)S(1)} %get-tuple-element.71), channel_id=1, source_target_pairs={{0,3},{1,0},{2,1},{3,2},{4,100},{5,101},{6,102},{7,103},{8,11},{9,... | collective-permute-start | bytes 1769480 | tf_op jit(solution)/shard_map/ppermute | solution.py:469
  131.3 14.5 %collective-permute-start.27 = (f32[40,768]{1,0:T(8,128)S(1)}, f32[40,768]{1,0:T(8,128)S(1)}, u32[]{:S(2)}, u32[]{:S(2)}) collective-permute-start(f32[40,768]{1,0:T(8,128)S(1)} %add_add_fusion.2), channel_id=1, source_target_pairs={{0,16},{1,17},{2,18},{3,19},{4,6},{5,7},{6,4},{7,5},{8,24},{9,25},... | collective-permute-start | bytes 368648 | tf_op jit(solution)/shard_map/ppermute | solution.py:469
  134.6 12.0 %collective-permute-start.28 = (f32[40,768]{1,0:T(8,128)S(1)}, f32[40,768]{1,0:T(8,128)S(1)}, u32[]{:S(2)}, u32[]{:S(2)}) collective-permute-start(f32[40,768]{1,0:T(8,128)S(1)} %add_add_fusion.2), channel_id=1, source_target_pairs={{0,8},{1,9},{2,10},{3,11},{4,5},{5,6},{6,7},{7,4},{8,16},{9,17},{1... | collective-permute-start | bytes 368648 | tf_op jit(solution)/shard_map/ppermute | solution.py:469
  134.6 13.8 %collective-permute-start.29 = (f32[40,768]{1,0:T(8,128)S(1)}, f32[40,768]{1,0:T(8,128)S(1)}, u32[]{:S(2)}, u32[]{:S(2)}) collective-permute-start(f32[40,768]{1,0:T(8,128)S(1)} %add_add_fusion.2), channel_id=1, source_target_pairs={{0,24},{1,25},{2,26},{3,27},{4,7},{5,4},{6,5},{7,6},{8,0},{9,1},{1... | collective-permute-start | bytes 368648 | tf_op jit(solution)/shard_map/ppermute | solution.py:469
  140.0 33.1 %collective-permute-start.3 = (bf16[2,16,1536]{2,1,0:T(8,128)(2,1)S(1)}, bf16[2,16,1536]{2,1,0:T(8,128)(2,1)S(1)}, u32[]{:S(2)}, u32[]{:S(2)}) collective-permute-start(bf16[2,16,1536]{2,1,0:T(8,128)(2,1)S(1)} %get-tuple-element.84), channel_id=1, source_target_pairs={{1,0},{2,1},{3,2},{5,4},{6,5},{7,6},{9,8},{10,9},{11,10},{13,12},{... | collective-permute-start | bytes 294920 | tf_op jit(solution)/shard_map/ppermute | solution.py:537
  142.1 9.2 %collective-permute-start.10 = (bf16[96,768]{1,0:T(8,128)(2,1)S(1)}, bf16[96,768]{1,0:T(8,128)(2,1)S(1)}, u32[]{:S(2)}, u32[]{:S(2)}) collective-permute-start(bf16[96,768]{1,0:T(8,128)(2,1)S(1)} %get-tuple-element.73), channel_id=1, source_target_pairs={{0,16},{1,17},{2,18},{3,19},{4,6},{5,7},{6,4},{7,5},{8,24},{9,25},... | collective-permute-start | bytes 442376 | tf_op jit(solution)/shard_map/ppermute | solution.py:469
  145.8 5.9 %collective-permute-start.11 = (bf16[96,768]{1,0:T(8,128)(2,1)S(1)}, bf16[96,768]{1,0:T(8,128)(2,1)S(1)}, u32[]{:S(2)}, u32[]{:S(2)}) collective-permute-start(bf16[96,768]{1,0:T(8,128)(2,1)S(1)} %get-tuple-element.74), channel_id=1, source_target_pairs={{0,8},{1,9},{2,10},{3,11},{4,5},{5,6},{6,7},{7,4},{8,16},{9,17},{1... | collective-permute-start | bytes 442376 | tf_op jit(solution)/shard_map/ppermute | solution.py:469
  146.6 7.4 %collective-permute-start.12 = (bf16[96,768]{1,0:T(8,128)(2,1)S(1)}, bf16[96,768]{1,0:T(8,128)(2,1)S(1)}, u32[]{:S(2)}, u32[]{:S(2)}) collective-permute-start(bf16[96,768]{1,0:T(8,128)(2,1)S(1)} %get-tuple-element.75), channel_id=1, source_target_pairs={{0,24},{1,25},{2,26},{3,27},{4,7},{5,4},{6,5},{7,6},{8,0},{9,1},{1... | collective-permute-start | bytes 442376 | tf_op jit(solution)/shard_map/ppermute | solution.py:469
  148.5 6.5 %collective-permute-start.30 = (f32[40,768]{1,0:T(8,128)S(1)}, f32[40,768]{1,0:T(8,128)S(1)}, u32[]{:S(2)}, u32[]{:S(2)}) collective-permute-start(f32[40,768]{1,0:T(8,128)S(1)} %add_add_fusion.1), channel_id=1, source_target_pairs={{0,64},{1,65},{2,66},{3,67},{4,20},{5,21},{6,22},{7,23},{8,72},{9,... | collective-permute-start | bytes 368648 | tf_op jit(solution)/shard_map/ppermute | solution.py:469
  151.3 5.2 %collective-permute-start.31 = (f32[40,768]{1,0:T(8,128)S(1)}, f32[40,768]{1,0:T(8,128)S(1)}, u32[]{:S(2)}, u32[]{:S(2)}) collective-permute-start(f32[40,768]{1,0:T(8,128)S(1)} %add_add_fusion.1), channel_id=1, source_target_pairs={{0,32},{1,33},{2,34},{3,35},{4,12},{5,13},{6,14},{7,15},{8,40},{9,... | collective-permute-start | bytes 368648 | tf_op jit(solution)/shard_map/ppermute | solution.py:469
  151.6 6.2 %collective-permute-start.32 = (f32[40,768]{1,0:T(8,128)S(1)}, f32[40,768]{1,0:T(8,128)S(1)}, u32[]{:S(2)}, u32[]{:S(2)}) collective-permute-start(f32[40,768]{1,0:T(8,128)S(1)} %add_add_fusion.1), channel_id=1, source_target_pairs={{0,96},{1,97},{2,98},{3,99},{4,28},{5,29},{6,30},{7,31},{8,104},{9... | collective-permute-start | bytes 368648 | tf_op jit(solution)/shard_map/ppermute | solution.py:469
  154.1 14.2 %collective-permute-start.13 = (bf16[96,768]{1,0:T(8,128)(2,1)S(1)}, bf16[96,768]{1,0:T(8,128)(2,1)S(1)}, u32[]{:S(2)}, u32[]{:S(2)}) collective-permute-start(bf16[96,768]{1,0:T(8,128)(2,1)S(1)} %add_convert_fusion), channel_id=1, source_target_pairs={{0,64},{1,65},{2,66},{3,67},{4,20},{5,21},{6,22},{7,23},{8,72},{9,... | collective-permute-start | bytes 442376 | tf_op jit(solution)/shard_map/ppermute | solution.py:469
  155.0 13.3 %collective-permute-start.14 = (bf16[96,768]{1,0:T(8,128)(2,1)S(1)}, bf16[96,768]{1,0:T(8,128)(2,1)S(1)}, u32[]{:S(2)}, u32[]{:S(2)}) collective-permute-start(bf16[96,768]{1,0:T(8,128)(2,1)S(1)} %add_convert_fusion), channel_id=1, source_target_pairs={{0,32},{1,33},{2,34},{3,35},{4,12},{5,13},{6,14},{7,15},{8,40},{9,... | collective-permute-start | bytes 442376 | tf_op jit(solution)/shard_map/ppermute | solution.py:469
  156.5 11.8 %collective-permute-start.15 = (bf16[96,768]{1,0:T(8,128)(2,1)S(1)}, bf16[96,768]{1,0:T(8,128)(2,1)S(1)}, u32[]{:S(2)}, u32[]{:S(2)}) collective-permute-start(bf16[96,768]{1,0:T(8,128)(2,1)S(1)} %add_convert_fusion), channel_id=1, source_target_pairs={{0,96},{1,97},{2,98},{3,99},{4,28},{5,29},{6,30},{7,31},{8,104},{9... | collective-permute-start | bytes 442376 | tf_op jit(solution)/shard_map/ppermute | solution.py:469
  157.8 26.7 %collective-permute-start.33 = (f32[40,768]{1,0:T(8,128)S(1)}, f32[40,768]{1,0:T(8,128)S(1)}, u32[]{:S(2)}, u32[]{:S(2)}) collective-permute-start(f32[40,768]{1,0:T(8,128)S(1)} %add_multiply_fusion), channel_id=1, source_target_pairs={{0,4},{1,5},{2,6},{3,7},{4,0},{5,1},{6,2},{7,3},{8,12},{9,13},{10,... | collective-permute-start | bytes 368648 | tf_op jit(solution)/shard_map/ppermute | solution.py:465
  168.4 7.6 %collective-permute-start.16 = (f32[96,768]{1,0:T(8,128)S(1)}, f32[96,768]{1,0:T(8,128)S(1)}, u32[]{:S(2)}, u32[]{:S(2)}) collective-permute-start(f32[96,768]{1,0:T(8,128)S(1)} %add_add_fusion.refs_0_), channel_id=1, source_target_pairs={{0,8},{1,9},{2,10},{3,11},{4,36},{5,37},{6,38},{7,39},{8,16},{9,17... | collective-permute-start | bytes 884744 | tf_op jit(solution)/shard_map/ppermute | solution.py:469
  168.5 15.1 %collective-permute-start.17 = (f32[96,768]{1,0:T(8,128)S(1)}, f32[96,768]{1,0:T(8,128)S(1)}, u32[]{:S(2)}, u32[]{:S(2)}) collective-permute-start(f32[96,768]{1,0:T(8,128)S(1)} %add_add_fusion.refs_0_), channel_id=1, source_target_pairs={{0,16},{1,17},{2,18},{3,19},{4,68},{5,69},{6,70},{7,71},{8,24},{9,... | collective-permute-start | bytes 884744 | tf_op jit(solution)/shard_map/ppermute | solution.py:469
  173.0 10.6 %collective-permute-start.18 = (f32[96,768]{1,0:T(8,128)S(1)}, f32[96,768]{1,0:T(8,128)S(1)}, u32[]{:S(2)}, u32[]{:S(2)}) collective-permute-start(f32[96,768]{1,0:T(8,128)S(1)} %add_add_fusion.refs_0_), channel_id=1, source_target_pairs={{0,24},{1,25},{2,26},{3,27},{4,100},{5,101},{6,102},{7,103},{8,0},... | collective-permute-start | bytes 884744 | tf_op jit(solution)/shard_map/ppermute | solution.py:469
  173.1 12.8 %collective-permute-start.19 = (f32[96,768]{1,0:T(8,128)S(1)}, f32[96,768]{1,0:T(8,128)S(1)}, u32[]{:S(2)}, u32[]{:S(2)}) collective-permute-start(f32[96,768]{1,0:T(8,128)S(1)} %add_add_fusion.refs_0_), channel_id=1, source_target_pairs={{0,4},{1,5},{2,6},{3,7},{4,0},{5,1},{6,2},{7,3},{8,12},{9,13},{10,... | collective-permute-start | bytes 884744 | tf_op jit(solution)/shard_map/ppermute | solution.py:465
  176.0 9.8 %collective-permute-start.20 = (f32[96,768]{1,0:T(8,128)S(1)}, f32[96,768]{1,0:T(8,128)S(1)}, u32[]{:S(2)}, u32[]{:S(2)}) collective-permute-start(f32[96,768]{1,0:T(8,128)S(1)} %collective-permute-done.16.refs_1_), channel_id=1, source_target_pairs={{0,4},{1,5},{2,6},{3,7},{4,0},{5,1},{6,2},{7,3},{8,12},{9,13},{10,... | collective-permute-start | bytes 884744 | tf_op jit(solution)/shard_map/ppermute | solution.py:465
  (30 other events, 255.4 us)

commit v3 on v2

v3 whole, which is shorter than its diff:
```python
import functools
import math

import jax
import jax.numpy as jnp
import numpy as np
from jax import lax
from jax.experimental import pallas as pl
from jax.experimental.pallas import tpu as pltpu
from jax.sharding import PartitionSpec as P

EPSILON = 1e-05
TAPS = 31
HALF = TAPS // 2
ROWS = 128
EDGE = 16
WINDOW = ROWS + 2 * EDGE
POINTS = 256
BINS = POINTS // 2
f32, bf16 = jnp.float32, jnp.bfloat16


def tables():
    place = np.arange(POINTS)
    bins = np.arange(BINS)[:, None]
    cosines = math.sqrt(2.0 / POINTS) * np.cos(2 * np.pi * ((bins * place) % POINTS) / POINTS)
    sines = math.sqrt(2.0 / POINTS) * np.sin(2 * np.pi * ((bins * place) % POINTS) / POINTS)
    cosines[0] = 1.0 / math.sqrt(POINTS)
    sines[0] = (1.0 - 2.0 * (place % 2)) / math.sqrt(POINTS)
    basis = np.concatenate([cosines, sines])
    high = basis.astype(jnp.bfloat16)
    low = (basis - high.astype(np.float64)).astype(jnp.bfloat16)
    split = np.concatenate([high, low])
    lags = np.arange(TAPS) - HALF
    turn = 2 * np.pi * ((bins * lags) % POINTS) / POINTS
    real, imag = np.cos(turn), np.sin(turn)
    other = real.copy()
    other[0] = 1.0 - 2.0 * (np.abs(lags) % 2)
    spectrum = np.concatenate([real, imag, other]).astype(np.float32)
    gather = np.concatenate([real, other, -imag]).astype(np.float32)
    wide, deep = np.zeros((3 * BINS, 32), np.float32), np.zeros((32, 3 * BINS), np.float32)
    wide[:, :TAPS], deep[:TAPS] = spectrum, gather.T
    return split, np.ascontiguousarray(split.T), wide, deep


def gapped(lengths_ref, lane, first, shape, dim, skip):
    row = lax.broadcasted_iota(jnp.int32, shape, dim) + skip
    frame = first + row
    place, end = row, 0
    for utter in range(lengths_ref.shape[1] - 1):
        end = end + lengths_ref[lane, utter]
        place = place + jnp.where(frame >= end, jnp.where(first < end, HALF, 0), 0)
    return place


def chosen_columns(split, place):
    count = place.shape[1]
    one_hot = (lax.broadcasted_iota(jnp.int32, (POINTS, count), 0) == place).astype(f32).astype(bf16)
    return jnp.dot(split, one_hot, preferred_element_type=f32).astype(bf16)


def chosen_rows(split_t, place):
    count = place.shape[0]
    one_hot = (lax.broadcasted_iota(jnp.int32, (count, POINTS), 1) == place).astype(f32).astype(bf16)
    return jnp.dot(one_hot, split_t, preferred_element_type=f32).astype(bf16)


def dot(a, b):
    return jnp.dot(a, b, preferred_element_type=f32)


def sigmoid(a):
    return 0.5 * jnp.tanh(0.5 * a) + 0.5


def forward_kernel(lane, blocks, meta_ref, lengths_ref, x_ref, before_ref, after_ref, split_ref, split_t_ref, spec_ref,
                   sw_ref, turned_ref, normed_ref, istd_ref, xhat_ref, win, conv):
    block = pl.program_id(0)
    total, channels = x_ref.shape
    first = meta_ref[0] + block * ROWS - EDGE
    start = (lane * blocks + block) * ROWS
    own = pl.ds(pl.multiple_of(block * ROWS, ROWS), ROWS)
    win[EDGE : EDGE + ROWS] = x_ref[pl.ds(pl.multiple_of(start, ROWS), ROWS)]
    halo = slice(lane * EDGE, (lane + 1) * EDGE)
    ahead = x_ref[pl.ds(pl.multiple_of(jnp.maximum(start - EDGE, 0), EDGE), EDGE)]
    behind = x_ref[pl.ds(pl.multiple_of(jnp.minimum(start + ROWS, total - EDGE), EDGE), EDGE)]
    win[:EDGE] = jnp.where(block == 0, before_ref[halo], ahead)
    win[EDGE + ROWS :] = jnp.where(block == blocks - 1, after_ref[halo], behind)
    into = chosen_columns(split_ref[...], gapped(lengths_ref, lane, first, (1, WINDOW), 1, 0))
    back = chosen_rows(split_t_ref[...], gapped(lengths_ref, lane, first, (ROWS, 1), 0, EDGE))
    spectra = pl.ds(pl.multiple_of(block * POINTS, POINTS), POINTS)
    width = 512
    for at in range(0, channels, width):
        cols = slice(at, at + width)
        rows = win[:, cols]
        xhat = dot(into[:POINTS], rows) + dot(into[POINTS:], rows)
        xhat_ref[spectra, cols] = xhat.astype(bf16)
        real, imag = xhat[:BINS], xhat[BINS:]
        p, q, other = spec_ref[:BINS, cols], spec_ref[BINS:POINTS, cols], spec_ref[POINTS : 3 * BINS, cols]
        zed = jnp.concatenate([real * p + imag * q, imag * other - real * q]).astype(bf16)
        conv[:, cols] = dot(back[:, :POINTS], zed) + dot(back[:, POINTS:], zed)
    gain, bias = spec_ref[3 * BINS : 3 * BINS + 1], spec_ref[3 * BINS + 1 : 3 * BINS + 2]
    strip = 16
    for at in range(0, ROWS, strip):
        rows = slice(at, at + strip)
        place = pl.ds(pl.multiple_of(block * ROWS + at, strip), strip)
        value = conv[rows]
        centred = value - jnp.sum(value, axis=1, keepdims=True) * (1.0 / channels)
        variance = jnp.sum(centred * centred, axis=1, keepdims=True) * (1.0 / channels)
        inv_std = lax.rsqrt(variance + EPSILON)
        normed = centred * inv_std
        affine = normed * gain + bias
        sw_ref[place] = (affine * sigmoid(affine)).astype(bf16)
        normed_ref[place] = normed
        istd_ref[place] = jnp.broadcast_to(inv_std, (strip, istd_ref.shape[1]))
    turned_ref[:, own] = sw_ref[own].T


def backward_kernel(lane, blocks, meta_ref, lengths_ref, cot_ref, sw_ref, normed_ref, istd_ref, xhat_ref, w_ref,
                    split_ref, split_t_ref, spec_ref, gather_ref, carry_ref, *rest):
    layer_ref, gi_ref, edge_ref, small_ref, gs, g, acc, sums, pending, tail = rest[-10:]
    block = pl.program_id(0)
    channels = cot_ref.shape[1]
    length = blocks * ROWS
    first = meta_ref[0] + block * ROWS - EDGE
    is_first, is_last = block == 0, block == blocks - 1

    @pl.when(is_first)
    def _():
        acc[...] = jnp.zeros_like(acc)
        sums[...] = jnp.zeros_like(sums)
        pending[...] = jnp.zeros_like(pending)
        tail[...] = jnp.zeros_like(tail)
        gs[...] = lax.dot_general(
            cot_ref[lane * length : (lane + 1) * length],
            w_ref[...],
            (((1,), (1,)), ((), ())),
            preferred_element_type=f32,
        )

    own = pl.ds(pl.multiple_of(block * ROWS, ROWS), ROWS)
    layer_ref[...] = dot(sw_ref[own], w_ref[...]).astype(bf16)
    gain, bias = spec_ref[3 * BINS : 3 * BINS + 1], spec_ref[3 * BINS + 1 : 3 * BINS + 2]
    strip = 16
    for at in range(0, ROWS, strip):
        place = pl.ds(pl.multiple_of(block * ROWS + at, strip), strip)
        normed = normed_ref[place]
        affine = normed * gain + bias
        gate = sigmoid(affine)
        grad = gs[place] * gate * (1.0 + affine * (1.0 - gate))
        prod = grad * normed
        sums[:8] += prod[:8] + prod[8:]
        sums[8:] += grad[:8] + grad[8:]
        grad_normed = grad * gain
        mean = jnp.sum(grad_normed, axis=1, keepdims=True) * (1.0 / channels)
        along = jnp.sum(grad_normed * normed, axis=1, keepdims=True) * (1.0 / channels)
        out = (istd_ref[place, :1] * (grad_normed - mean - normed * along)).astype(bf16)
        g[at : at + strip] = out
        g[ROWS + at : ROWS + at + strip] = out
    into = chosen_columns(split_ref[...], gapped(lengths_ref, lane, first, (1, ROWS), 1, EDGE))
    into = jnp.concatenate([into[:POINTS], into[POINTS:]], axis=1)
    back = chosen_rows(split_t_ref[...], gapped(lengths_ref, lane, first, (WINDOW, 1), 0, 0))
    base = pl.multiple_of(block * ROWS, ROWS)
    early = pl.ds(pl.multiple_of(jnp.maximum(base - EDGE, 0), EDGE), EDGE)
    cosines = pl.ds(pl.multiple_of(block * POINTS, POINTS), BINS)
    sines = pl.ds(pl.multiple_of(block * POINTS + BINS, BINS), BINS)
    width = 256
    for at in range(0, channels, width):
        cols = slice(at, at + width)
        ghat = dot(into, g[:, cols])
        cg, sg = ghat[:BINS], ghat[BINS:]
        cx, sx = xhat_ref[cosines, cols].astype(f32), xhat_ref[sines, cols].astype(f32)
        acc[:BINS, cols] += cg * cx
        acc[BINS:POINTS, cols] += sg * sx
        acc[POINTS:, cols] += sg * cx - cg * sx
        p, q, other = spec_ref[:BINS, cols], spec_ref[BINS:POINTS, cols], spec_ref[POINTS : 3 * BINS, cols]
        vee = jnp.concatenate([cg * p - sg * q, sg * other + cg * q]).astype(bf16)
        part = dot(back[:, :POINTS], vee) + dot(back[:, POINTS:], vee)
        head, out = part[:EDGE], part[EDGE : EDGE + ROWS]
        gi_ref[early, cols] = (pending[:, cols] + head).astype(bf16)
        gi_ref[pl.ds(base, EDGE), cols] = (out[:EDGE] + tail[:, cols]).astype(bf16)
        gi_ref[pl.ds(base + EDGE, ROWS - EDGE), cols] = out[EDGE:].astype(bf16)
        edge_ref[:EDGE, cols] = jnp.where(is_first, head.astype(bf16), edge_ref[:EDGE, cols])
        edge_ref[EDGE:, cols] = part[EDGE + ROWS :].astype(bf16)
        pending[:, cols] = out[ROWS - EDGE :]
        tail[:, cols] = part[EDGE + ROWS :]

    @pl.when(is_last)
    def _():
        table_high, table_low = halves(gather_ref[...])
        wide = 512
        for at in range(0, channels, wide):
            cols = slice(at, at + wide)
            high, low = halves(acc[:, cols])
            value = dot(table_high, high) + dot(table_low, high) + dot(table_high, low)
            small_ref[:32, cols] = value + carry_ref[:32, cols]
        prod, grad = sums[:8], sums[8:]
        small_ref[32:40] = carry_ref[32:40] + jnp.concatenate(
            [
                jnp.sum(prod, axis=0, keepdims=True),
                jnp.sum(grad, axis=0, keepdims=True),
                jnp.zeros((6, channels), f32),
            ]
        )


def halves(value):
    high = value.astype(bf16)
    return high, (value - high.astype(f32)).astype(bf16)


def spectrum_kernel(table_ref, kernel_ref, gain_ref, bias_ref, spec_ref):
    channels = kernel_ref.shape[1]
    table_high, table_low = halves(table_ref[...])
    taps = jnp.concatenate([kernel_ref[...], jnp.zeros((32 - TAPS, channels), f32)])
    high, low = halves(taps)
    spec_ref[: 3 * BINS] = dot(table_high, high) + dot(table_low, high) + dot(table_high, low)
    spec_ref[3 * BINS :] = jnp.concatenate(
        [gain_ref[...].reshape(1, channels), bias_ref[...].reshape(1, channels), jnp.zeros((6, channels), f32)]
    )


def outer_kernel(meta_ref, sw0_ref, sw1_ref, sw2_ref, cot_ref, other_ref, acc_ref):
    rows = sw0_ref.shape[1]
    share = acc_ref.shape[0] // 4
    cols = pl.ds(pl.multiple_of(meta_ref[1] * acc_ref.shape[1], acc_ref.shape[1]), acc_ref.shape[1])
    for at in range(4):
        part = slice(at * share, (at + 1) * share)
        acc_ref[part] = (
            dot(sw0_ref[part], cot_ref[:rows, cols])
            + dot(sw1_ref[part], cot_ref[rows:, cols])
            + dot(sw2_ref[part], other_ref[:rows, cols])
        )


def last_outer_kernel(meta_ref, acc_ref, sw_ref, cot_ref, own_ref, one_ref, two_ref, three_ref, total):
    share, width = acc_ref.shape[0] // 4, acc_ref.shape[1]
    piece = share // 4
    rows = sw_ref.shape[1]
    cols = pl.ds(pl.multiple_of(meta_ref[1] * width, width), width)
    for at in range(4):
        part = slice(at * share, (at + 1) * share)
        total[part] = acc_ref[part] + dot(sw_ref[part], cot_ref[rows:, cols])
    core, place = meta_ref[1], meta_ref[2]
    for shift, ref in enumerate((own_ref, one_ref, two_ref, three_ref)):
        chunk = lax.rem(place + shift, 4)
        for k in range(4):
            start = jnp.where(core == 0, chunk * share + k * piece, k * share + chunk * piece)
            value = total[pl.ds(pl.multiple_of(start, piece), piece)]
            ref[k * piece : (k + 1) * piece] = value.astype(ref.dtype)


def first_sum_kernel(meta_ref, a_ref, b_ref, c_ref, d_ref, own_ref, one_ref, two_ref, three_ref):
    piece = own_ref.shape[0]
    for shift, ref in enumerate((own_ref, one_ref, two_ref, three_ref)):
        rows = pl.ds(pl.multiple_of(lax.rem(meta_ref[3] + shift, 4) * piece, piece), piece)
        value = (a_ref[rows] + c_ref[rows].astype(f32)) + (b_ref[rows].astype(f32) + d_ref[rows].astype(f32))
        ref[...] = value.astype(ref.dtype)


def place_kernel(scale, meta_ref, *refs):
    out_ref = refs[-1]
    width = refs[0].shape[1]
    piece = out_ref.shape[0] // 4
    for side in range(2):
        core = meta_ref[1] if side == 0 else 1 - meta_ref[1]
        place = meta_ref[4] if side == 0 else meta_ref[5]
        cols = pl.ds(pl.multiple_of(core * width, width), width)
        for shift in range(4):
            rows = pl.ds(pl.multiple_of(lax.rem(place + 4 - shift, 4) * piece, piece), piece)
            out_ref[rows, cols] = refs[side * 4 + shift][:piece] * scale


def place_small_kernel(scale, meta_ref, own_ref, away_ref, taps_ref, gain_ref, bias_ref):
    first = meta_ref[1] == 0
    width = own_ref.shape[1]
    own, away = own_ref[...] * scale, away_ref[...] * scale
    for side in range(2):
        cols = slice(side * width, (side + 1) * width)
        value = jnp.where(first == (side == 0), own, away)
        taps_ref[:, cols] = value[:TAPS]
        gain_ref[cols] = value[32]
        bias_ref[cols] = value[33]


def whole(shape):
    return pl.BlockSpec(shape, lambda *i: (0,) * len(shape))


SMEM = pl.BlockSpec(memory_space=pltpu.SMEM)
VMEM = pl.BlockSpec(memory_space=pltpu.VMEM)


def params(mebibytes):
    return pltpu.CompilerParams(vmem_limit_bytes=mebibytes << 20)


def cost(flops, moved):
    return pl.CostEstimate(flops=flops, bytes_accessed=moved, transcendentals=0)


def near(*arrays):
    return [pltpu.with_memory_space_constraint(a, pltpu.VMEM) for a in arrays]


def forward(lane, meta, lengths, flat, before, after, split, split_t, spec, interpret=False):
    total, channels = flat.shape
    lanes = lengths.shape[0]
    length = total // lanes
    blocks = length // ROWS
    return pl.pallas_call(
        functools.partial(forward_kernel, lane, blocks),
        grid=(blocks,),
        in_specs=[SMEM, SMEM] + [VMEM] * 6,
        out_specs=[VMEM] * 5,
        out_shape=[
            pltpu.VMEM((length, channels), bf16),
            pltpu.VMEM((channels, length), bf16),
            pltpu.VMEM((length, channels), f32),
            pltpu.VMEM((length, 128), f32),
            pltpu.VMEM((blocks * POINTS, channels), bf16),
        ],
        scratch_shapes=[pltpu.VMEM((WINDOW, channels), bf16), pltpu.VMEM((ROWS, channels), f32)],
        compiler_params=params(12),
        cost_estimate=cost(length * channels * 2000, length * channels * 12),
        interpret=interpret,
        name=f"conv_norm_swish_{lane}",
    )(meta, lengths, *near(flat, before, after, split, split_t, spec))


def backward(lane, meta, lengths, cot, sw, normed, istd, xhat, w, split, split_t, spec, gather, carry, layer, gi,
             interpret=False):
    total, channels = cot.shape
    length = sw.shape[0]
    blocks = length // ROWS
    at = lane * blocks
    kept = [] if layer is None else [layer, gi]
    return pl.pallas_call(
        functools.partial(backward_kernel, lane, blocks),
        grid=(blocks,),
        in_specs=[SMEM, SMEM] + [VMEM] * 11 + [pl.BlockSpec(memory_space=pl.ANY)] * len(kept),
        out_specs=[
            pl.BlockSpec((ROWS, channels), lambda i: (i + at, 0)),
            pl.BlockSpec((length, channels), lambda i: (lane, 0)),
            VMEM,
            VMEM,
        ],
        out_shape=[
            jax.ShapeDtypeStruct((total, channels), bf16),
            jax.ShapeDtypeStruct((total, channels), bf16),
            pltpu.VMEM((2 * EDGE, channels), bf16),
            pltpu.VMEM((40, channels), f32),
        ],
        scratch_shapes=[
            pltpu.VMEM((length, channels), f32),
            pltpu.VMEM((2 * ROWS, channels), bf16),
            pltpu.VMEM((3 * BINS, channels), f32),
            pltpu.VMEM((16, channels), f32),
            pltpu.VMEM((EDGE, channels), f32),
            pltpu.VMEM((EDGE, channels), f32),
        ],
        input_output_aliases={13: 0, 14: 1} if kept else {},
        compiler_params=params(20),
        cost_estimate=cost(length * channels * 8000, length * channels * 20),
        interpret=interpret,
        name=f"backward_{lane}",
    )(meta, lengths, *near(cot, sw, normed, istd, xhat, w, split, split_t, spec, gather, carry), *kept)


def outer(meta, sw0, sw1, sw2, cot, other, interpret=False):
    channels, rows = sw0.shape
    width = channels // 2
    return pl.pallas_call(
        outer_kernel,
        in_specs=[SMEM] + [VMEM] * 5,
        out_specs=VMEM,
        out_shape=pltpu.VMEM((channels, width), f32),
        compiler_params=params(12),
        cost_estimate=cost(6 * rows * channels * width, 10 * rows * channels),
        interpret=interpret,
        name="outer_most",
    )(meta, *near(sw0, sw1, sw2, cot, other))


def last_outer(meta, acc, sw, cot, interpret=False):
    channels, rows = sw.shape
    width, share = channels // 2, channels // 4
    return pl.pallas_call(
        last_outer_kernel,
        in_specs=[SMEM] + [VMEM] * 3,
        out_specs=[VMEM] * 4,
        out_shape=[pltpu.VMEM((share, width), d) for d in (f32, bf16, bf16, bf16)],
        scratch_shapes=[pltpu.VMEM(acc.shape, f32)],
        compiler_params=params(12),
        cost_estimate=cost(2 * rows * channels * width, 10 * rows * channels),
        interpret=interpret,
        name="outer_last",
    )(meta, *near(acc, sw, cot))


def first_sum(meta, parts):
    share, width = parts[0].shape
    piece = share // 4
    return pl.pallas_call(
        first_sum_kernel,
        in_specs=[SMEM] + [VMEM] * 4,
        out_specs=[VMEM] * 4,
        out_shape=[pltpu.VMEM((piece, width), d) for d in (f32, bf16, bf16, bf16)],
        compiler_params=params(12),
        name="sum_first",
    )(meta, *near(*parts))


def place(meta, pieces, share, scale):
    width = pieces[0].shape[1]
    return pl.pallas_call(
        functools.partial(place_kernel, scale),
        in_specs=[SMEM] + [VMEM] * 8,
        out_specs=VMEM,
        out_shape=jax.ShapeDtypeStruct((share, 2 * width), f32),
        compiler_params=params(12),
        name="place",
    )(meta, *near(*pieces))


def place_small(meta, own, away, scale):
    width = own.shape[1]
    return pl.pallas_call(
        functools.partial(place_small_kernel, scale),
        in_specs=[SMEM] + [VMEM] * 2,
        out_specs=[VMEM] * 3,
        out_shape=[
            jax.ShapeDtypeStruct((TAPS, 2 * width), f32),
            jax.ShapeDtypeStruct((2 * width,), f32),
            jax.ShapeDtypeStruct((2 * width,), f32),
        ],
        compiler_params=params(12),
        name="place_small",
    )(meta, own, away)


def shifts(size):
    up = [(i, i + 1) for i in range(size - 1)]
    return up, [(j, i) for i, j in up]


EVERY = ("dp", "seq")


def along(axes, shift):
    pairs = []
    for device in range(128):
        where = {"y": device % 4, "c": device // 4 % 2, "x": device // 8 % 4, "z": device // 32}
        axis = axes[where["c"]]
        moved = dict(where)
        moved[axis] = (where[axis] + shift) % (2 if axis == "c" else 4)
        pairs.append((device, ((moved["z"] * 4 + moved["x"]) * 2 + moved["c"]) * 4 + moved["y"]))
    return pairs


def swap(value):
    return lax.ppermute(value, EVERY, along("cc", 1))


def spread(values, axes):
    return [lax.ppermute(value, EVERY, along(axes, s + 1)) for s, value in enumerate(values)]


def four(own, one, two, three):
    own, one, two, three = (v.astype(f32) for v in (own, one, two, three))
    return (own + two) + (one + three)


def all_four(value, axes):
    return four(value, *spread([value] * 3, axes))


def both(value):
    return jnp.concatenate(halves(value))


def joined(value):
    rows = value.shape[0] // 2
    return value[:rows].astype(f32) + value[rows:].astype(f32)


def local(glu_out, lengths, kernel, norm_gain, norm_bias, w_out, cotangent, interpret=False):
    lanes, length, channels = glu_out.shape
    seq_count = lax.axis_size("seq")
    norm_scale = 1.0 / math.sqrt(lanes * lax.axis_size("dp") * length * seq_count)
    y = lax.axis_index("seq")
    dp = lax.axis_index("dp")
    core, x, z = lax.rem(dp, 2), lax.rem(lax.div(dp, 2), 4), lax.div(dp, 8)
    first = core == 0
    meta = jnp.stack(
        [
            y * length,
            core,
            jnp.where(first, y, z),
            jnp.where(first, x, y),
            jnp.where(first, x, z),
            jnp.where(first, z, x),
        ]
    ).astype(jnp.int32)
    up, down = shifts(seq_count)
    before = lax.ppermute(glu_out[:, length - EDGE :], "seq", up).reshape(lanes * EDGE, channels)
    after = lax.ppermute(glu_out[:, :EDGE], "seq", down).reshape(lanes * EDGE, channels)
    cot = cotangent.reshape(-1, channels)
    split, split_t, wide, deep = (jnp.asarray(t) for t in tables())
    spec = pl.pallas_call(
        spectrum_kernel,
        in_specs=[VMEM] * 4,
        out_specs=VMEM,
        out_shape=pltpu.VMEM((3 * BINS + 8, channels), f32),
        compiler_params=params(12),
        interpret=interpret,
        name="spectrum",
    )(wide, kernel, norm_gain, norm_bias)
    flat = glu_out.reshape(lanes * length, channels)
    ahead = [
        forward(lane, meta, lengths, flat, before, after, split, split_t, spec, interpret=interpret)
        for lane in range(lanes)
    ]
    turned = [a[1] for a in ahead]
    share, half = channels // seq_count, channels // 2
    whole_slice = lax.axis_size("dp") == 32
    if whole_slice:
        cot_other = swap(cot)
        other = [swap(t) for t in turned]
        acc = outer(meta, turned[0], turned[1], other[0], cot, cot_other)
        parts = list(last_outer(meta, acc, other[1], cot_other))
        sent = spread(parts[1:], "yz")
        cot, parts[0] = lax.optimization_barrier((cot, parts[0]))
    else:
        grad_w = lax.psum(dot(jnp.concatenate(turned, axis=1), cot), "seq") * norm_scale
        grad_w = lax.dynamic_slice_in_dim(grad_w, y * share, share, 0)
    small, layer, gi, edges = jnp.zeros((40, channels), f32), None, None, []
    for lane in range(lanes):
        sw, _, normed, istd, xhat = ahead[lane]
        layer, gi, edge, small = backward(
            lane, meta, lengths, cot, sw, normed, istd, xhat, w_out, split, split_t, spec, deep, small, layer, gi,
            interpret=interpret,
        )
        edges.append(edge)
    heads = jnp.concatenate([e[:EDGE] for e in edges])
    tails = jnp.concatenate([e[EDGE:] for e in edges])
    if whole_slice:
        small = small + swap(small)
        small = both(lax.dynamic_slice_in_dim(small, core * half, half, 1))
        flat_small = jnp.concatenate([small[:40], small[40:]], axis=1)
        ways = [jnp.concatenate([tails, flat_small]), flat_small, jnp.concatenate([heads, flat_small])]
        one, two, three = spread(ways, "yy")
        count = lanes * EDGE
        before, after = one[:count], three[:count]

        def split_rows(v):
            return jnp.concatenate([v[:, :half], v[:, half:]])

        small = four(joined(small), *(joined(split_rows(v)) for v in (one[count:], two, three[count:])))
        pieces = first_sum(meta, [parts[0]] + sent)
        pieces = [pieces[0]] + spread(pieces[1:], "xy")
        piece = four(*pieces).astype(bf16)
        rows = piece.shape[0]
        sent = jnp.concatenate([piece, both(small)])
        got = [sent] + spread([sent] * 3, "zx")
        piece = four(*(v[:rows] for v in got))
        small = four(*(joined(v[rows:]) for v in got))
        sent = jnp.concatenate([piece, small])
        got = [sent] + spread([sent] * 3, "xz")
        small = four(*(v[rows:] for v in got))
        grad_w = place(meta, got + [swap(v[:rows]) for v in got], share, norm_scale)
        taps, gain, bias = place_small(meta, small, swap(small), norm_scale)
    else:
        before, after = lax.ppermute(tails, "seq", up), lax.ppermute(heads, "seq", down)
        small = lax.psum(small, "seq") * norm_scale
        taps, gain, bias = small[:TAPS], small[32], small[33]
    before = jnp.where(y == 0, 0.0, before.astype(f32)).astype(bf16).reshape(lanes, EDGE, channels)
    after = jnp.where(y == seq_count - 1, 0.0, after.astype(f32)).astype(bf16).reshape(lanes, EDGE, channels)
    gi = gi.reshape(lanes, length, channels)
    gi = gi.at[:, :EDGE].add(before).at[:, length - EDGE :].add(after)
    return (layer.reshape(lanes, length, channels), gi, grad_w, taps, gain, bias)


def solution(mesh):
    in_specs = (P("dp", "seq", None), P("dp", None), P(), P(), P(), P(), P("dp", "seq", None))
    out_specs = (P("dp", "seq", None), P("dp", "seq", None), P("seq", None), P(), P(), P())
    return jax.shard_map(local, mesh=mesh, in_specs=in_specs, out_specs=out_specs, check_vma=False)
```

time: 189 us -> 176 us (0.931)
  waiting for transfers between devices: 7.54 us -> 20.5 us
  Pallas kernels: 81.9 us -> 69.7 us
  starting transfers between devices: 69.3 us -> 60.6 us
  other arithmetic: 7.29 us -> 3.59 us
    pallas_call x2, Pallas kernels: 48.5 us -> 32.4 us  [backward(): pl.pallas_call(functools.partial(backward_kernel, lane, blocks), grid=(bl...]
    ppermute x21 -> x15, waiting for transfers between devices: 7.5 us -> 19.2 us  [spread(): lax.ppermute(value, EVERY, along(axes, s + 1))]
    ppermute x21 -> x15, starting transfers between devices: 34.9 us -> 25 us  [spread(): lax.ppermute(value, EVERY, along(axes, s + 1))]
    ppermute x9, starting transfers between devices: 24.2 us -> 31 us  [swap(): return lax.ppermute(value, EVERY, along('cc', 1))]
    ppermute x2 -> x0, starting transfers between devices: 5.5 us -> none  [the longest x1 4.22 us: local(): from_before = lax.ppermute(edge[:, EDGE:], 'seq', up)]
    another operation x3 -> x0, other arithmetic: 4.62 us -> none  [the longest x1 1.94 us: local(): layer = jnp.stack([b[0] for b in back])]
    scatter-add x2, other arithmetic: 0.08 us -> 3.13 us  [local(): gi = gi.at[:, :EDGE].add(before).at[:, length - EDGE:].add(after)]
    pallas_call x2, Pallas kernels: 17.8 us -> 20.4 us  [forward(): pl.pallas_call(functools.partial(forward_kernel, lane, blocks), grid=(blo...]
  transfers between devices with their start and end apart: 34 -> 26, of which waited for: 4 -> 8; matrix products, arithmetic and copies ran while one was open for 6% -> 3% of each run, Pallas kernels for 42% -> 17%
where the time goes in v3:
time: 176 us
  Pallas kernels  69.7 us (40%)
  starting transfers between devices  60.6 us (34%)
  waiting for transfers between devices  20.5 us (12%)
  local copies, waits for them, and re-layouts  20.4 us (12%)
  other arithmetic  3.59 us (2%)
    pallas_call x2, Pallas kernels, backward(): pl.pallas_call(functools.partial(backward_kernel, lane, blocks), grid=(bl...  32.4 us
    ppermute x9, starting transfers between devices, swap(): return lax.ppermute(value, EVERY, along('cc', 1))  31 us
    ppermute x15, starting transfers between devices, spread(): lax.ppermute(value, EVERY, along(axes, s + 1))  25 us
    pallas_call x2, Pallas kernels, forward(): pl.pallas_call(functools.partial(forward_kernel, lane, blocks), grid=(blo...  20.4 us
    unnamed x64, local copies, waits for them, and re-layouts  19.3 us
    ppermute x15, waiting for transfers between devices, spread(): lax.ppermute(value, EVERY, along(axes, s + 1))  19.2 us
    pallas_call x1, Pallas kernels, outer(): pl.pallas_call(outer_kernel, in_specs=[SMEM] + [VMEM] * 5, out_specs=VMEM...  7.32 us
    pallas_call x1, Pallas kernels, last_outer(): pl.pallas_call(last_outer_kernel, in_specs=[SMEM] + [VMEM] * 3, out_specs...  4.21 us
  transfers between devices with their start and end apart: 26, of which 8 were waited for; matrix products, arithmetic and copies ran while one was open for 3% of the time, Pallas kernels for 17%

profile of v3, /device:TPU:1, one launch (start us, length us, event | category | flops | bytes accessed | tf_op | source)
XLA Modules:
  0.0 175.8 jit_solution(13955525555353722293)
XLA Ops:
  0.7 1.5 collective-permute-start.3
  3.1 3.3 %collective-permute-start = (bf16[2,16,1536]{2,1,0:T(8,128)(2,1)S(1)}, bf16[2,16,1536]{2,1,0:T(8,128)(2,1)S(1)}, u32[]{:S(2)}, u32[]{:S(2)}) collective-permute-start(bf16[2,16,1536]{2,1,0:T(8,128)(2,1)S(1)} %get-tuple-element.97), channel_id=1, source_target_pairs={{0,1},{1,2},{2,3},{4,5},{5,6},{6,7},{8,9},{9,10},{10,11},{12,13},{... | collective-permute-start | bytes 294920 | tf_op jit(solution)/shard_map/ppermute | solution.py:506
  12.4 1.9 %copy-done = bf16[2,512,1536]{2,1,0:T(8,128)(2,1)S(1)} copy-done((bf16[2,512,1536]{2,1,0:T(8,128)(2,1)S(1)}, bf16[2,512,1536]{2,1,0:T(8,128)(2,1)}, u32[]{:S(2)}) %copy-start) | copy-done | bytes 3145752
  14.9 10.2 %conv_norm_swish_0.1 = (bf16[512,1536]{1,0:T(8,128)(2,1)S(1)}, bf16[1536,512]{1,0:T(8,128)(2,1)}, f32[512,1536]{1,0:T(8,128)S(1)}, f32[512,128]{1,0:T(8,128)S(1)}, bf16[1024,1536]{1,0:T(8,128)(2,1)S(1)}) custom-call(s32[6]{0:T(128)S(1)} %stack.27.meta_ref, s32[2,8]{1,0:T(2,128)S(1)} %copy-done.17, bf16[1024,1536]{1,0:T(8,128)(2,1)S(1)} %bitcast.14, ...), custom_call_target="tpu_custom_call" | custom-call | flops 1572864000 | bytes 9437184 | tf_op jit(solution)/shard_map/conv_norm_swish_0/pallas_call | solution.py:311
  25.1 1.7 copy-done.21
  26.8 1.7 copy-done.23
  30.8 10.2 %conv_norm_swish_1.1 = (bf16[512,1536]{1,0:T(8,128)(2,1)S(1)}, bf16[1536,512]{1,0:T(8,128)(2,1)}, f32[512,1536]{1,0:T(8,128)S(1)}, f32[512,128]{1,0:T(8,128)S(1)}, bf16[1024,1536]{1,0:T(8,128)(2,1)S(1)}) custom-call(s32[6]{0:T(128)S(1)} %stack.27.meta_ref, s32[2,8]{1,0:T(2,128)S(1)} %copy-done.18, bf16[1024,1536]{1,0:T(8,128)(2,1)S(1)} %bitcast.15, ...), custom_call_target="tpu_custom_call" | custom-call | flops 1572864000 | bytes 9437184 | tf_op jit(solution)/shard_map/conv_norm_swish_1/pallas_call | solution.py:311
  41.0 1.6 copy-done.4
  42.6 1.7 copy-done.6
  45.5 1.9 %copy-done.1 = bf16[2,512,1536]{2,1,0:T(8,128)(2,1)S(1)} copy-done((bf16[2,512,1536]{2,1,0:T(8,128)(2,1)S(1)}, bf16[2,512,1536]{2,1,0:T(8,128)(2,1)}, u32[]{:S(2)}) %copy-start.1) | copy-done | bytes 3145752
  47.4 7.3 %outer_most.1.acc_ref = f32[1536,768]{1,0:T(8,128)S(1)} custom-call(s32[6]{0:T(128)S(1)} %stack.27.meta_ref, bf16[1536,512]{1,0:T(8,128)(2,1)} %get-tuple-element.61.sw0_ref, bf16[1536,512]{1,0:T(8,128)(2,1)} %get-tuple-element.62.sw1_ref, bf16[1536,512]{1,0:T(8,128)(2,1)} %collective-permute-done.2.sw2_ref, bf16[1024,1536]{1,0:T(8,128)(2,1)S(1)} %bitcast.17, ...), custom_call_target="tpu_custom_call" | custom-call | flops 3623878656 | bytes 7864320 | tf_op jit(solution)/shard_map/outer_most/pallas_call | solution.py:373
  54.8 4.2 %outer_last.1 = (f32[384,768]{1,0:T(8,128)S(1)}, bf16[384,768]{1,0:T(8,128)(2,1)S(1)}, bf16[384,768]{1,0:T(8,128)(2,1)S(1)}, bf16[384,768]{1,0:T(8,128)(2,1)S(1)}) custom-call(s32[6]{0:T(128)S(1)} %stack.27.meta_ref, f32[1536,768]{1,0:T(8,128)S(1)} %outer_most.1.acc_ref, bf16[1536,512]{1,0:T(8,128)(2,1)} %collective-permute-done.4.sw_ref, ...), custom_call_target="tpu_custom_call" | custom-call | flops 1207959552 | bytes 7864320 | tf_op jit(solution)/shard_map/outer_last/pallas_call | solution.py:388
  61.7 16.3 %backward_0.1 = (bf16[1024,1536]{1,0:T(8,128)(2,1)}, bf16[1024,1536]{1,0:T(8,128)(2,1)}, bf16[32,1536]{1,0:T(8,128)(2,1)S(1)}, f32[40,1536]{1,0:T(8,128)S(1)}) custom-call(s32[6]{0:T(128)S(1)} %stack.27.meta_ref, s32[2,8]{1,0:T(2,128)S(1)} %copy-done.18, bf16[1024,1536]{1,0:T(8,128)(2,1)S(1)} %bitcast.18, bf16[512,1536]{1,0:T(8,128)(2,1)S(1)} %copy-done.26, ...), custom_call_target="tpu_custom_call" | custom-call | flops 6291456000 | bytes 15728640 | tf_op jit(solution)/shard_map/backward_0/pallas_call | solution.py:338
  78.0 16.1 %backward_1.1 = (bf16[1024,1536]{1,0:T(8,128)(2,1)}, bf16[1024,1536]{1,0:T(8,128)(2,1)}, bf16[32,1536]{1,0:T(8,128)(2,1)S(1)}, f32[40,1536]{1,0:T(8,128)S(1)}) custom-call(s32[6]{0:T(128)S(1)} %stack.27.meta_ref, s32[2,8]{1,0:T(2,128)S(1)} %copy-done.18, bf16[1024,1536]{1,0:T(8,128)(2,1)S(1)} %bitcast.19, ...), custom_call_target="tpu_custom_call", output_to_operand_aliasing={{0}: (13, {}), {1}: (14, {})} | custom-call | flops 6291456000 | bytes 15728640 | tf_op jit(solution)/shard_map/backward_1/pallas_call | solution.py:338
  95.7 1.4 collective-permute-start.6
  97.1 1.5 collective-permute-start.7
  98.7 1.6 collective-permute-start.14
  100.3 3.8 %collective-permute-start.10 = (bf16[384,768]{1,0:T(8,128)(2,1)}, bf16[384,768]{1,0:T(8,128)(2,1)S(1)}, u32[]{:S(2)}, u32[]{:S(2)}) collective-permute-start(bf16[384,768]{1,0:T(8,128)(2,1)} %copy-done.29), channel_id=1, source_target_pairs={{0,3},{1,0},{2,1},{3,2},{4,100},{5,101},{6,102},{7,103},{8,11},{9,... | collective-permute-start | bytes 1769480 | tf_op jit(solution)/shard_map/ppermute | solution.py:466
  104.1 3.5 %collective-permute-done.14 = bf16[40,1536]{1,0:T(8,128)(2,1)S(1)} collective-permute-done((bf16[40,1536]{1,0:T(8,128)(2,1)S(1)}, bf16[40,1536]{1,0:T(8,128)(2,1)S(1)}, u32[]{:S(2)}, u32[]{:S(2)}) %collective-permute-start.14) | collective-permute-done | bytes 122912 | tf_op jit(solution)/shard_map/ppermute | solution.py:466
  107.6 3.6 %collective-permute-start.9 = (bf16[384,768]{1,0:T(8,128)(2,1)}, bf16[384,768]{1,0:T(8,128)(2,1)S(1)}, u32[]{:S(2)}, u32[]{:S(2)}) collective-permute-start(bf16[384,768]{1,0:T(8,128)(2,1)} %copy-done.27), channel_id=1, source_target_pairs={{0,2},{1,3},{2,0},{3,1},{4,68},{5,69},{6,70},{7,71},{8,10},{9,11},... | collective-permute-start | bytes 1769480 | tf_op jit(solution)/shard_map/ppermute | solution.py:466
  111.3 9.6 %collective-permute-done.8.b_ref = bf16[384,768]{1,0:T(8,128)(2,1)S(1)} collective-permute-done((bf16[384,768]{1,0:T(8,128)(2,1)}, bf16[384,768]{1,0:T(8,128)(2,1)S(1)}, u32[]{:S(2)}, u32[]{:S(2)}) %collective-permute-start.8) | collective-permute-done | bytes 589856 | tf_op jit(solution)/shard_map/ppermute | solution.py:466
  123.1 2.4 %collective-permute-start.13 = (bf16[96,768]{1,0:T(8,128)(2,1)S(1)}, bf16[96,768]{1,0:T(8,128)(2,1)S(1)}, u32[]{:S(2)}, u32[]{:S(2)}) collective-permute-start(bf16[96,768]{1,0:T(8,128)(2,1)S(1)} %get-tuple-element.88), channel_id=1, source_target_pairs={{0,24},{1,25},{2,26},{3,27},{4,7},{5,4},{6,5},{7,6},{8,0},{9,1},{1... | collective-permute-start | bytes 442376 | tf_op jit(solution)/shard_map/ppermute | solution.py:466
  125.6 2.0 %collective-permute-done.11 = bf16[96,768]{1,0:T(8,128)(2,1)S(1)} collective-permute-done((bf16[96,768]{1,0:T(8,128)(2,1)S(1)}, bf16[96,768]{1,0:T(8,128)(2,1)S(1)}, u32[]{:S(2)}, u32[]{:S(2)}) %collective-permute-start.11) | collective-permute-done | bytes 147488 | tf_op jit(solution)/shard_map/ppermute | solution.py:466
  129.0 2.8 %collective-permute-start.15 = (bf16[176,768]{1,0:T(8,128)(2,1)S(1)}, bf16[176,768]{1,0:T(8,128)(2,1)S(1)}, u32[]{:S(2)}, u32[]{:S(2)}) collective-permute-start(bf16[176,768]{1,0:T(8,128)(2,1)S(1)} %pad_maximum_fusion.1), channel_id=1, source_target_pairs={{0,64},{1,65},{2,66},{3,67},{4,20},{5,21},{6,22},{7,23},{8,72},{9,... | collective-permute-start | bytes 811016 | tf_op jit(solution)/shard_map/ppermute | solution.py:466
  132.1 2.4 %collective-permute-start.17 = (bf16[176,768]{1,0:T(8,128)(2,1)S(1)}, bf16[176,768]{1,0:T(8,128)(2,1)S(1)}, u32[]{:S(2)}, u32[]{:S(2)}) collective-permute-start(bf16[176,768]{1,0:T(8,128)(2,1)S(1)} %pad_maximum_fusion.1), channel_id=1, source_target_pairs={{0,96},{1,97},{2,98},{3,99},{4,28},{5,29},{6,30},{7,31},{8,104},{9... | collective-permute-start | bytes 811016 | tf_op jit(solution)/shard_map/ppermute | solution.py:466
  134.5 1.6 fusion.8
  136.0 2.7 %collective-permute-done.16 = bf16[176,768]{1,0:T(8,128)(2,1)S(1)} collective-permute-done((bf16[176,768]{1,0:T(8,128)(2,1)S(1)}, bf16[176,768]{1,0:T(8,128)(2,1)S(1)}, u32[]{:S(2)}, u32[]{:S(2)}) %collective-permute-start.16) | collective-permute-done | bytes 270368 | tf_op jit(solution)/shard_map/ppermute | solution.py:466
  139.1 2.9 %collective-permute-start.19 = (f32[136,768]{1,0:T(8,128)S(1)}, f32[136,768]{1,0:T(8,128)S(1)}, u32[]{:S(2)}, u32[]{:S(2)}) collective-permute-start(f32[136,768]{1,0:T(8,128)S(1)} %pad_maximum_fusion.refs_0_), channel_id=1, source_target_pairs={{0,16},{1,17},{2,18},{3,19},{4,68},{5,69},{6,70},{7,71},{8,24},{9,... | collective-permute-start | bytes 1253384 | tf_op jit(solution)/shard_map/ppermute | solution.py:466
  142.8 16.7 %collective-permute-start.21 = (f32[96,768]{1,0:T(8,128)S(1)}, f32[96,768]{1,0:T(8,128)S(1)}, u32[]{:S(2)}, u32[]{:S(2)}) collective-permute-start(f32[96,768]{1,0:T(8,128)S(1)} %add_add_fusion), channel_id=1, source_target_pairs={{0,4},{1,5},{2,6},{3,7},{4,0},{5,1},{6,2},{7,3},{8,12},{9,13},{10,... | collective-permute-start | bytes 884744 | tf_op jit(solution)/shard_map/ppermute | solution.py:462
  159.5 10.5 %collective-permute-start.25 = (f32[40,768]{1,0:T(8,128)S(1)}, f32[40,768]{1,0:T(8,128)S(1)}, u32[]{:S(2)}, u32[]{:S(2)}) collective-permute-start(f32[40,768]{1,0:T(8,128)S(1)} %fusion.6.own_ref), channel_id=1, source_target_pairs={{0,4},{1,5},{2,6},{3,7},{4,0},{5,1},{6,2},{7,3},{8,12},{9,13},{10,... | collective-permute-start | bytes 368648 | tf_op jit(solution)/shard_map/ppermute | solution.py:462
  170.8 1.6 fusion.7
  173.7 2.2 %place.1 = f32[384,1536]{1,0:T(8,128)} custom-call(s32[6]{0:T(128)S(1)} %stack.27.meta_ref, f32[136,768]{1,0:T(8,128)S(1)} %pad_maximum_fusion.refs_0_, f32[136,768]{1,0:T(8,128)S(1)} %collective-permute-done.18.refs_1_, f32[136,768]{1,0:T(8,128)S(1)} %collective-permute-done.19.refs_2_, f32[136,768]{1,0:T(8,128)S(1)} %collective-permute-done.20.refs_3_, ...), custom_call_target="tpu_custom_call" | custom-call | tf_op jit(solution)/shard_map/place/pallas_call | solution.py:416
  (116 shorter events, 22.6 us)
Async XLA Ops:
  0.7 44.8 %collective-permute-start.3 = (bf16[1024,1536]{1,0:T(8,128)(2,1)}, bf16[1024,1536]{1,0:T(8,128)(2,1)}, u32[]{:S(2)}, u32[]{:S(2)}) collective-permute-start(bf16[1024,1536]{1,0:T(8,128)(2,1)} %bitcast.16), channel_id=1, source_target_pairs={{0,4},{1,5},{2,6},{3,7},{4,0},{5,1},{6,2},{7,3},{8,12},{9,13},{10,... | collective-permute-start | bytes 9437192 | tf_op jit(solution)/shard_map/ppermute | solution.py:462
  3.1 9.0 %collective-permute-start = (bf16[2,16,1536]{2,1,0:T(8,128)(2,1)S(1)}, bf16[2,16,1536]{2,1,0:T(8,128)(2,1)S(1)}, u32[]{:S(2)}, u32[]{:S(2)}) collective-permute-start(bf16[2,16,1536]{2,1,0:T(8,128)(2,1)S(1)} %get-tuple-element.97), channel_id=1, source_target_pairs={{0,1},{1,2},{2,3},{4,5},{5,6},{6,7},{8,9},{9,10},{10,11},{12,13},{... | collective-permute-start | bytes 294920 | tf_op jit(solution)/shard_map/ppermute | solution.py:506
  6.4 5.9 %collective-permute-start.1 = (bf16[2,16,1536]{2,1,0:T(8,128)(2,1)S(1)}, bf16[2,16,1536]{2,1,0:T(8,128)(2,1)S(1)}, u32[]{:S(2)}, u32[]{:S(2)}) collective-permute-start(bf16[2,16,1536]{2,1,0:T(8,128)(2,1)S(1)} %get-tuple-element.96), channel_id=1, source_target_pairs={{1,0},{2,1},{3,2},{5,4},{6,5},{7,6},{9,8},{10,9},{11,10},{13,12},{... | collective-permute-start | bytes 294920 | tf_op jit(solution)/shard_map/ppermute | solution.py:507
  12.1 18.7 %copy-start.18 = (s32[2,8]{1,0:T(2,128)S(1)}, s32[2,8]{1,0:T(2,128)}, u32[]{:S(2)}) copy-start(s32[2,8]{1,0:T(2,128)} %lengths_ref.7) | copy-start | bytes 196
  29.6 15.9 %collective-permute-start.2 = (bf16[1536,512]{1,0:T(8,128)(2,1)}, bf16[1536,512]{1,0:T(8,128)(2,1)}, u32[]{:S(2)}, u32[]{:S(2)}) collective-permute-start(bf16[1536,512]{1,0:T(8,128)(2,1)} %get-tuple-element.61.sw0_ref), channel_id=1, source_target_pairs={{0,4},{1,5},{2,6},{3,7},{4,0},{5,1},{6,2},{7,3},{8,12},{9,13},{10,... | collective-permute-start | bytes 4718600 | tf_op jit(solution)/shard_map/ppermute | solution.py:462
  45.5 9.3 %collective-permute-start.4 = (bf16[1536,512]{1,0:T(8,128)(2,1)}, bf16[1536,512]{1,0:T(8,128)(2,1)}, u32[]{:S(2)}, u32[]{:S(2)}) collective-permute-start(bf16[1536,512]{1,0:T(8,128)(2,1)} %get-tuple-element.62.sw1_ref), channel_id=1, source_target_pairs={{0,4},{1,5},{2,6},{3,7},{4,0},{5,1},{6,2},{7,3},{8,12},{9,13},{10,... | collective-permute-start | bytes 4718600 | tf_op jit(solution)/shard_map/ppermute | solution.py:462
  61.5 16.4 %copy-start.12 = (f32[384,768]{1,0:T(8,128)}, f32[384,768]{1,0:T(8,128)S(1)}, u32[]{:S(2)}) copy-start(f32[384,768]{1,0:T(8,128)S(1)} %get-tuple-element.81.a_ref) | copy-start | bytes 3538948
  61.6 16.3 %copy-start.5 = (f32[512,1536]{1,0:T(8,128)S(1)}, f32[512,1536]{1,0:T(8,128)}, u32[]{:S(2)}) copy-start(f32[512,1536]{1,0:T(8,128)} %copy-done.4) | copy-start | bytes 9437188
  61.6 16.3 %copy-start.7 = (bf16[1024,1536]{1,0:T(8,128)(2,1)S(1)}, bf16[1024,1536]{1,0:T(8,128)(2,1)}, u32[]{:S(2)}) copy-start(bf16[1024,1536]{1,0:T(8,128)(2,1)} %copy-done.6) | copy-start | bytes 9437188
  61.7 16.3 %copy-start.11 = (bf16[512,1536]{1,0:T(8,128)(2,1)S(1)}, bf16[512,1536]{1,0:T(8,128)(2,1)}, u32[]{:S(2)}) copy-start(bf16[512,1536]{1,0:T(8,128)(2,1)} %copy-done.10) | copy-start | bytes 4718596
  94.1 26.7 %copy-start.13 = (f32[384,768]{1,0:T(8,128)S(1)}, f32[384,768]{1,0:T(8,128)}, u32[]{:S(2)}) copy-start(f32[384,768]{1,0:T(8,128)} %copy-done.12) | copy-start | bytes 3538948
  94.1 1.5 collective-permute-start.5
  95.7 15.5 %collective-permute-start.6 = (bf16[72,1536]{1,0:T(8,128)(2,1)S(1)}, bf16[72,1536]{1,0:T(8,128)(2,1)S(1)}, u32[]{:S(2)}, u32[]{:S(2)}) collective-permute-start(bf16[72,1536]{1,0:T(8,128)(2,1)S(1)} %get-tuple-element.99), channel_id=1, source_target_pairs={{0,1},{1,2},{2,3},{3,0},{4,5},{5,6},{6,7},{7,4},{8,9},{9,10},{10,1... | collective-permute-start | bytes 663560 | tf_op jit(solution)/shard_map/ppermute | solution.py:466
  97.1 14.0 %collective-permute-start.7 = (bf16[72,1536]{1,0:T(8,128)(2,1)S(1)}, bf16[72,1536]{1,0:T(8,128)(2,1)S(1)}, u32[]{:S(2)}, u32[]{:S(2)}) collective-permute-start(bf16[72,1536]{1,0:T(8,128)(2,1)S(1)} %get-tuple-element.98), channel_id=1, source_target_pairs={{0,3},{1,0},{2,1},{3,2},{4,7},{5,4},{6,5},{7,6},{8,11},{9,8},{10,9... | collective-permute-start | bytes 663560 | tf_op jit(solution)/shard_map/ppermute | solution.py:466
  98.7 8.9 %collective-permute-start.14 = (bf16[40,1536]{1,0:T(8,128)(2,1)S(1)}, bf16[40,1536]{1,0:T(8,128)(2,1)S(1)}, u32[]{:S(2)}, u32[]{:S(2)}) collective-permute-start(bf16[40,1536]{1,0:T(8,128)(2,1)S(1)} %pad_maximum_fusion.3), channel_id=1, source_target_pairs={{0,2},{1,3},{2,0},{3,1},{4,6},{5,7},{6,4},{7,5},{8,10},{9,11},{10,... | collective-permute-start | bytes 368648 | tf_op jit(solution)/shard_map/ppermute | solution.py:466
  100.3 11.0 %collective-permute-start.10 = (bf16[384,768]{1,0:T(8,128)(2,1)}, bf16[384,768]{1,0:T(8,128)(2,1)S(1)}, u32[]{:S(2)}, u32[]{:S(2)}) collective-permute-start(bf16[384,768]{1,0:T(8,128)(2,1)} %copy-done.29), channel_id=1, source_target_pairs={{0,3},{1,0},{2,1},{3,2},{4,100},{5,101},{6,102},{7,103},{8,11},{9,... | collective-permute-start | bytes 1769480 | tf_op jit(solution)/shard_map/ppermute | solution.py:466
  104.1 16.8 %collective-permute-start.8 = (bf16[384,768]{1,0:T(8,128)(2,1)}, bf16[384,768]{1,0:T(8,128)(2,1)S(1)}, u32[]{:S(2)}, u32[]{:S(2)}) collective-permute-start(bf16[384,768]{1,0:T(8,128)(2,1)} %copy-done.28), channel_id=1, source_target_pairs={{0,1},{1,2},{2,3},{3,0},{4,36},{5,37},{6,38},{7,39},{8,9},{9,10},{... | collective-permute-start | bytes 1769480 | tf_op jit(solution)/shard_map/ppermute | solution.py:466
  107.6 13.3 %collective-permute-start.9 = (bf16[384,768]{1,0:T(8,128)(2,1)}, bf16[384,768]{1,0:T(8,128)(2,1)S(1)}, u32[]{:S(2)}, u32[]{:S(2)}) collective-permute-start(bf16[384,768]{1,0:T(8,128)(2,1)} %copy-done.27), channel_id=1, source_target_pairs={{0,2},{1,3},{2,0},{3,1},{4,68},{5,69},{6,70},{7,71},{8,10},{9,11},... | collective-permute-start | bytes 1769480 | tf_op jit(solution)/shard_map/ppermute | solution.py:466
  121.7 5.9 %collective-permute-start.11 = (bf16[96,768]{1,0:T(8,128)(2,1)S(1)}, bf16[96,768]{1,0:T(8,128)(2,1)S(1)}, u32[]{:S(2)}, u32[]{:S(2)}) collective-permute-start(bf16[96,768]{1,0:T(8,128)(2,1)S(1)} %get-tuple-element.86), channel_id=1, source_target_pairs={{0,16},{1,17},{2,18},{3,19},{4,6},{5,7},{6,4},{7,5},{8,24},{9,25},... | collective-permute-start | bytes 442376 | tf_op jit(solution)/shard_map/ppermute | solution.py:466
  122.9 6.0 %collective-permute-start.12 = (bf16[96,768]{1,0:T(8,128)(2,1)S(1)}, bf16[96,768]{1,0:T(8,128)(2,1)S(1)}, u32[]{:S(2)}, u32[]{:S(2)}) collective-permute-start(bf16[96,768]{1,0:T(8,128)(2,1)S(1)} %get-tuple-element.87), channel_id=1, source_target_pairs={{0,8},{1,9},{2,10},{3,11},{4,5},{5,6},{6,7},{7,4},{8,16},{9,17},{1... | collective-permute-start | bytes 442376 | tf_op jit(solution)/shard_map/ppermute | solution.py:466
  123.1 5.7 %collective-permute-start.13 = (bf16[96,768]{1,0:T(8,128)(2,1)S(1)}, bf16[96,768]{1,0:T(8,128)(2,1)S(1)}, u32[]{:S(2)}, u32[]{:S(2)}) collective-permute-start(bf16[96,768]{1,0:T(8,128)(2,1)S(1)} %get-tuple-element.88), channel_id=1, source_target_pairs={{0,24},{1,25},{2,26},{3,27},{4,7},{5,4},{6,5},{7,6},{8,0},{9,1},{1... | collective-permute-start | bytes 442376 | tf_op jit(solution)/shard_map/ppermute | solution.py:466
  129.0 7.1 %collective-permute-start.15 = (bf16[176,768]{1,0:T(8,128)(2,1)S(1)}, bf16[176,768]{1,0:T(8,128)(2,1)S(1)}, u32[]{:S(2)}, u32[]{:S(2)}) collective-permute-start(bf16[176,768]{1,0:T(8,128)(2,1)S(1)} %pad_maximum_fusion.1), channel_id=1, source_target_pairs={{0,64},{1,65},{2,66},{3,67},{4,20},{5,21},{6,22},{7,23},{8,72},{9,... | collective-permute-start | bytes 811016 | tf_op jit(solution)/shard_map/ppermute | solution.py:466
  131.8 7.0 %collective-permute-start.16 = (bf16[176,768]{1,0:T(8,128)(2,1)S(1)}, bf16[176,768]{1,0:T(8,128)(2,1)S(1)}, u32[]{:S(2)}, u32[]{:S(2)}) collective-permute-start(bf16[176,768]{1,0:T(8,128)(2,1)S(1)} %pad_maximum_fusion.1), channel_id=1, source_target_pairs={{0,32},{1,33},{2,34},{3,35},{4,12},{5,13},{6,14},{7,15},{8,40},{9,... | collective-permute-start | bytes 811016 | tf_op jit(solution)/shard_map/ppermute | solution.py:466
  132.1 6.7 %collective-permute-start.17 = (bf16[176,768]{1,0:T(8,128)(2,1)S(1)}, bf16[176,768]{1,0:T(8,128)(2,1)S(1)}, u32[]{:S(2)}, u32[]{:S(2)}) collective-permute-start(bf16[176,768]{1,0:T(8,128)(2,1)S(1)} %pad_maximum_fusion.1), channel_id=1, source_target_pairs={{0,96},{1,97},{2,98},{3,99},{4,28},{5,29},{6,30},{7,31},{8,104},{9... | collective-permute-start | bytes 811016 | tf_op jit(solution)/shard_map/ppermute | solution.py:466
  139.0 20.5 %collective-permute-start.18 = (f32[136,768]{1,0:T(8,128)S(1)}, f32[136,768]{1,0:T(8,128)S(1)}, u32[]{:S(2)}, u32[]{:S(2)}) collective-permute-start(f32[136,768]{1,0:T(8,128)S(1)} %pad_maximum_fusion.refs_0_), channel_id=1, source_target_pairs={{0,8},{1,9},{2,10},{3,11},{4,36},{5,37},{6,38},{7,39},{8,16},{9,17... | collective-permute-start | bytes 1253384 | tf_op jit(solution)/shard_map/ppermute | solution.py:466
  139.1 20.4 %collective-permute-start.19 = (f32[136,768]{1,0:T(8,128)S(1)}, f32[136,768]{1,0:T(8,128)S(1)}, u32[]{:S(2)}, u32[]{:S(2)}) collective-permute-start(f32[136,768]{1,0:T(8,128)S(1)} %pad_maximum_fusion.refs_0_), channel_id=1, source_target_pairs={{0,16},{1,17},{2,18},{3,19},{4,68},{5,69},{6,70},{7,71},{8,24},{9,... | collective-permute-start | bytes 1253384 | tf_op jit(solution)/shard_map/ppermute | solution.py:466
  142.0 17.5 %collective-permute-start.20 = (f32[136,768]{1,0:T(8,128)S(1)}, f32[136,768]{1,0:T(8,128)S(1)}, u32[]{:S(2)}, u32[]{:S(2)}) collective-permute-start(f32[136,768]{1,0:T(8,128)S(1)} %pad_maximum_fusion.refs_0_), channel_id=1, source_target_pairs={{0,24},{1,25},{2,26},{3,27},{4,100},{5,101},{6,102},{7,103},{8,0},... | collective-permute-start | bytes 1253384 | tf_op jit(solution)/shard_map/ppermute | solution.py:466
  142.8 30.9 %collective-permute-start.21 = (f32[96,768]{1,0:T(8,128)S(1)}, f32[96,768]{1,0:T(8,128)S(1)}, u32[]{:S(2)}, u32[]{:S(2)}) collective-permute-start(f32[96,768]{1,0:T(8,128)S(1)} %add_add_fusion), channel_id=1, source_target_pairs={{0,4},{1,5},{2,6},{3,7},{4,0},{5,1},{6,2},{7,3},{8,12},{9,13},{10,... | collective-permute-start | bytes 884744 | tf_op jit(solution)/shard_map/ppermute | solution.py:462
  159.5 12.9 %collective-permute-start.25 = (f32[40,768]{1,0:T(8,128)S(1)}, f32[40,768]{1,0:T(8,128)S(1)}, u32[]{:S(2)}, u32[]{:S(2)}) collective-permute-start(f32[40,768]{1,0:T(8,128)S(1)} %fusion.6.own_ref), channel_id=1, source_target_pairs={{0,4},{1,5},{2,6},{3,7},{4,0},{5,1},{6,2},{7,3},{8,12},{9,13},{10,... | collective-permute-start | bytes 368648 | tf_op jit(solution)/shard_map/ppermute | solution.py:462
  170.0 3.6 %collective-permute-start.22 = (f32[96,768]{1,0:T(8,128)S(1)}, f32[96,768]{1,0:T(8,128)S(1)}, u32[]{:S(2)}, u32[]{:S(2)}) collective-permute-start(f32[96,768]{1,0:T(8,128)S(1)} %slice.200), channel_id=1, source_target_pairs={{0,4},{1,5},{2,6},{3,7},{4,0},{5,1},{6,2},{7,3},{8,12},{9,13},{10,... | collective-permute-start | bytes 884744 | tf_op jit(solution)/shard_map/ppermute | solution.py:462
  170.1 3.5 %collective-permute-start.23 = (f32[96,768]{1,0:T(8,128)S(1)}, f32[96,768]{1,0:T(8,128)S(1)}, u32[]{:S(2)}, u32[]{:S(2)}) collective-permute-start(f32[96,768]{1,0:T(8,128)S(1)} %slice.201), channel_id=1, source_target_pairs={{0,4},{1,5},{2,6},{3,7},{4,0},{5,1},{6,2},{7,3},{8,12},{9,13},{10,... | collective-permute-start | bytes 884744 | tf_op jit(solution)/shard_map/ppermute | solution.py:462
  170.7 2.9 %collective-permute-start.24 = (f32[96,768]{1,0:T(8,128)S(1)}, f32[96,768]{1,0:T(8,128)S(1)}, u32[]{:S(2)}, u32[]{:S(2)}) collective-permute-start(f32[96,768]{1,0:T(8,128)S(1)} %slice.202), channel_id=1, source_target_pairs={{0,4},{1,5},{2,6},{3,7},{4,0},{5,1},{6,2},{7,3},{8,12},{9,13},{10,... | collective-permute-start | bytes 884744 | tf_op jit(solution)/shard_map/ppermute | solution.py:462
  (26 other events, 124.0 us)
